TPU v7x, 128 devices: a whole 4x4x4 slice. The times are simulated.
128 devices in a mesh: region: 16 (over z, y), sub: 8 (over x, core).
Axes of the slice: x: 4, y: 4, z: 4, core: 2. Of those that a mesh axis runs over, the one named last changes fastest.
Arguments:
- tokens: bfloat16 [131072, 1024], P(('region', 'sub')), may hold values from -6 to 6
- nodes: bfloat16 [20480, 1024], P(('region', 'sub')), may hold values from -6 to 6
- dests: int32 [131072, 2], P(('region', 'sub')), may hold values from 0 to 20479, as said below
- token_count: int32 [128], P(('region', 'sub')), may hold values from 256 to 1024, as said below
- w_src: bfloat16 [1024, 1024], replicated, may hold values from -0.1875 to 0.1875
- w_dst: bfloat16 [1024, 1024], replicated, may hold values from -0.1875 to 0.1875
- bias: float32 [1024], replicated, may hold values from -4 to 4
- w_out: bfloat16 [1024, 1024], replicated, may hold values from -0.1875 to 0.1875
- cotangent: bfloat16 [20480, 1024], P(('region', 'sub')), may hold values from -6 to 6
Outputs:
- updated: bfloat16 [20480, 1024], P(('region', 'sub'))
- token_grad: bfloat16 [131072, 1024], P(('region', 'sub'))
- node_grad: bfloat16 [20480, 1024], P(('region', 'sub'))
- grad_src: float32 [1024, 1024], P(('region', 'sub'))
- grad_dst: float32 [1024, 1024], P(('region', 'sub'))
- grad_out: float32 [1024, 1024], P(('region', 'sub'))
- grad_bias: float32 [1024], P(('region', 'sub'))
Inputs may be any that keep to these rules, and one draw needn't show every extreme that they name: `dests`: node block of device d (d = region index * 8 + sub index) is rows d * 160 to (d + 1) * 160 - 1. Every edge of a token of device (r, s) points into the node block of (r, s), (r - 1, s), (r + 1, s), (r, s - 1) or (r, s + 1), among those that exist. `token_count`: some device has all 1024 slots live.
All inputs are finite; a program needn't handle non-finite values.
Results may differ from a plain program's by a relative error of at most 0.012.
Values may be sent and summed in bfloat16 or wider, within the bound.
A program may use at most 128 MiB of HBM per device.

v0:
```python
import jax
import jax.numpy as jnp
from jax import lax
from jax.sharding import PartitionSpec as P


def with_halo(cells, sides, width):
    for axis, dim in sides:
        count = lax.axis_size(axis)
        ends = count - 1
        head = lax.slice_in_dim(cells, 0, width, axis=dim)
        tail = lax.slice_in_dim(cells, cells.shape[dim] - width, cells.shape[dim], axis=dim)
        cells = jnp.concatenate(
            [
                lax.ppermute(tail, axis, [(i, (i + 1) % count) for i in range(ends)]),
                cells,
                lax.ppermute(head, axis, [((i + 1) % count, i) for i in range(ends)]),
            ],
            axis=dim,
        )
    return cells


def from_behind(block, axis, distance):
    devices = range(lax.axis_size(axis))
    route = [(i - distance, i) for i in devices if i - distance in devices]
    return lax.ppermute(block, axis, route)


def contract_rows(left, right):
    return lax.dot_general(
        left, right, (((0,), (0,)), ((), ())), preferred_element_type=jnp.float32
    )


def contract_cols(left, right):
    return lax.dot_general(
        left, right, (((1,), (1,)), ((), ())), preferred_element_type=jnp.float32
    )


def body(tokens, nodes, dests, token_count, w_src, w_dst, bias, w_out, cotangent):
    f32 = jnp.float32
    bf16 = jnp.bfloat16
    tok_rows = tokens.shape[0]
    node_rows = nodes.shape[0]
    hidden = w_src.shape[1]
    block_rows = min(512, tok_rows)
    region_index = lax.axis_index("region")
    sub_index = lax.axis_index("sub")
    sub_size = lax.axis_size("sub")
    node_proj = jnp.dot(nodes, w_dst, preferred_element_type=f32).astype(bf16)
    node_up = contract_cols(cotangent, w_out).astype(bf16)
    stacked = jnp.concatenate([node_proj, node_up], axis=0).reshape(1, 1, 2 * node_rows, hidden)
    padded = with_halo(stacked, (("region", 0), ("sub", 1)), 1)
    nearby = jnp.stack([padded[1, 1], padded[0, 1], padded[2, 1], padded[1, 0], padded[1, 2]])
    near_proj = nearby[:, :node_rows].reshape(5 * node_rows, hidden)
    near_up = nearby[:, node_rows:].reshape(5 * node_rows, hidden)
    owner_block = dests // node_rows
    local_row = dests % node_rows
    delta_row = owner_block // sub_size - region_index
    delta_col = owner_block % sub_size - sub_index
    slot_index = jnp.where(
        delta_row == -1,
        1,
        jnp.where(
            delta_row == 1, 2, jnp.where(delta_col == -1, 3, jnp.where(delta_col == 1, 4, 0))
        ),
    )
    near_index = slot_index * node_rows + local_row
    live_count = token_count[0]
    n_blocks = (live_count + block_rows - 1) // block_rows
    columns = jnp.arange(5 * node_rows, dtype=jnp.int32)

    def one_block(block_index, state_tuple):
        seg_fwd, seg_bwd, grad_src, grad_bias, token_grad = state_tuple
        start = block_index * block_rows
        x_block = lax.dynamic_slice_in_dim(tokens, start, block_rows, 0)
        near_block = lax.dynamic_slice_in_dim(near_index, start, block_rows, 0)
        row_ids = start + jnp.arange(block_rows, dtype=jnp.int32)
        live_mask = (row_ids < live_count).astype(f32)[:, None, None]
        token_proj = jnp.dot(x_block, w_src, preferred_element_type=f32)
        preact = token_proj[:, None, :] + jnp.take(near_proj, near_block, axis=0).astype(f32) + bias
        sigma = jax.nn.sigmoid(preact)
        edge_act = (preact * sigma * live_mask).astype(bf16)
        upstream = jnp.take(near_up, near_block, axis=0).astype(f32)
        edge_grad = (upstream * sigma * (1.0 + preact * (1.0 - sigma)) * live_mask).astype(bf16)
        onehot = (near_block.reshape(-1)[:, None] == columns[None, :]).astype(bf16)
        seg_fwd = seg_fwd + contract_rows(onehot, edge_act.reshape(-1, hidden))
        seg_bwd = seg_bwd + contract_rows(onehot, edge_grad.reshape(-1, hidden))
        grad_wide = edge_grad.astype(f32)
        token_back = jnp.sum(grad_wide, axis=1).astype(bf16)
        x_grad = contract_cols(token_back, w_src).astype(bf16)
        token_grad = lax.dynamic_update_slice_in_dim(token_grad, x_grad, start, 0)
        grad_src = grad_src + contract_rows(x_block, token_back)
        grad_bias = grad_bias + jnp.sum(grad_wide, axis=(0, 1))
        return (seg_fwd, seg_bwd, grad_src, grad_bias, token_grad)

    start_state = (
        jnp.zeros((5 * node_rows, hidden), f32),
        jnp.zeros((5 * node_rows, hidden), f32),
        jnp.zeros(w_src.shape, f32),
        jnp.zeros((hidden,), f32),
        jnp.zeros(tokens.shape, bf16),
    )
    seg_fwd, seg_bwd, grad_src, grad_bias, token_grad = lax.fori_loop(
        0, n_blocks, one_block, start_state
    )
    partials = jnp.concatenate(
        [
            seg_fwd.astype(bf16).reshape(5, node_rows, hidden),
            seg_bwd.astype(bf16).reshape(5, node_rows, hidden),
        ],
        axis=1,
    )
    summed = partials[0].astype(f32)
    for offset, slot_pick in ((1, 2), (-1, 1)):
        summed = summed + from_behind(partials[slot_pick], "region", offset).astype(f32)
    for offset, slot_pick in ((1, 4), (-1, 3)):
        summed = summed + from_behind(partials[slot_pick], "sub", offset).astype(f32)
    node_sum = summed[:node_rows].astype(bf16)
    node_back = summed[node_rows:].astype(bf16)
    updated = (nodes.astype(f32) + jnp.dot(node_sum, w_out, preferred_element_type=f32)).astype(
        bf16
    )
    node_grad = (cotangent.astype(f32) + contract_cols(node_back, w_dst)).astype(bf16)
    grad_dst = contract_rows(nodes, node_back)
    grad_out = contract_rows(node_sum, cotangent)
    part_src, part_dst, part_out, part_bias = (
        lax.psum_scatter(grad_src, ("region", "sub"), scatter_dimension=0, tiled=True),
        lax.psum_scatter(grad_dst, ("region", "sub"), scatter_dimension=0, tiled=True),
        lax.psum_scatter(grad_out, ("region", "sub"), scatter_dimension=0, tiled=True),
        lax.psum_scatter(grad_bias, ("region", "sub"), scatter_dimension=0, tiled=True),
    )
    return (updated, token_grad, node_grad, part_src, part_dst, part_out, part_bias)


def solution(mesh):
    return jax.shard_map(
        body,
        mesh=mesh,
        in_specs=(
            P(("region", "sub"), None),
            P(("region", "sub"), None),
            P(("region", "sub"), None),
            P(("region", "sub")),
            P(),
            P(),
            P(),
            P(),
            P(("region", "sub"), None),
        ),
        out_specs=(
            P(("region", "sub"), None),
            P(("region", "sub"), None),
            P(("region", "sub"), None),
            P(("region", "sub"), None),
            P(("region", "sub"), None),
            P(("region", "sub"), None),
            P(("region", "sub")),
        ),
        check_vma=False,
    )
```

profile of v0, /device:TPU:1, one launch (start us, length us, event | category | flops | bytes accessed | tf_op | source)
XLA Modules:
  0.0 2153.2 jit_solution(7611254897006592238)
XLA Ops:
  7.2 1.5 copy-done
  8.8 2.0 convolution_convert_fusion.1
  11.4 4.1 collective-permute-start
  16.7 12.0 collective-permute-done
  28.8 3.8 collective-permute-done.1
  32.6 1.5 pad_maximum_fusion
  34.1 4.9 collective-permute-start.2
  39.0 1.9 collective-permute-start.3
  44.8 3.3 fusion.34
  49.3 11.6 collective-permute-done.2
  62.0 3.3 collective-permute-done.3
  66.4 2.3 fusion.44
  68.7 2.5 broadcast_in_dim.34
  71.2 2.1 broadcast.45
  73.3 2.2 broadcast.45.clone
  75.5 1.6 broadcast_in_dim.36
  77.1 76.6 %while.21 = (s32[]{:T(128)}, f32[800,1024]{1,0:T(8,128)}, f32[800,1024]{1,0:T(8,128)}, f32[1024,1024]{1,0:T(8,128)}, f32[1024]{0:T(1024)S(1)}, /*index=5*/bf16[1...) while((s32[]{:T(128)}, f32[800,1024]{1,0:T(8,128)}, ...), condition=%wide.region_3.5_spmd.clone, body=%wide.region_0.4_spmd.clone.sunk | while | flops 6604074496 | bytes 126439816 | solution.py:106
  78.3 7.6 gather_fusion
  86.0 4.1 reshape.111
  90.1 7.6 gather_fusion.1
  97.8 4.1 reshape.112
  101.9 4.5 fusion.81
  107.2 6.3 convert_reduce_fusion.2
  113.5 1.4 copy-done.1
  114.8 3.5 copy.77
  118.3 4.1 reshape.114
  122.6 6.5 fusion.83
  129.1 3.5 copy.76
  132.6 4.1 reshape.113
  136.7 6.2 fusion.82
  143.0 2.2 reduce_sum.30
  145.2 5.9 convolution_add_fusion.4
  151.1 1.3 fusion.84
  152.4 1.3 copy-done.13
  153.8 2.3 convert_element_type.96
  157.2 3.2 collective-permute-start.4
  161.7 78.6 %collective-permute-start.6 = (bf16[320,1024]{1,0:T(8,128)(2,1)S(1)}, bf16[320,1024]{1,0:T(8,128)(2,1)S(1)}, u32[]{:S(2)}, u32[]{:S(2)}) collective-permute-start(bf16[320,1024]{1,0:T(8,128)(2,1)S(1)} %get-tuple-element.309), channel_id=1, source_target_pairs={{0,1},{1,2},{2,3},{3,4},{4,5},{5,6},{6,7},{8,9},{9,10},{10,11},{11... | collective-permute-start | bytes 1966088 | tf_op jit(solution)/shard_map/ppermute | solution.py:27
  240.4 2.1 collective-permute-start.7
  242.4 5.8 collective-permute-done.5
  248.3 4.4 collective-permute-done.7
  253.3 2.7 convolution_bitcast_fusion
  256.0 5.4 copy.59
  262.4 2.7 fusion.41
  265.2 70.3 %all-reduce = f32[1024]{0:T(1024)S(1)} all-reduce(f32[1024]{0:T(1024)S(1)} %get-tuple-element.204), channel_id=5, replica_groups=mesh['region'=16,'sub'=8] {'region','sub'}, use_global_device_ids=true, to_apply=%region_7.9.clone | all-reduce | flops 1024 | bytes 8192
  337.3 1.6 fusion.20
  338.8 529.4 %reduce-scatter.6.cloned.1.call-done = f32[8,1024]{1,0:T(8,128)} async-done(((f32[1024,1024]{1,0:T(8,128)}), f32[8,1024]{1,0:T(8,128)}) %reduce-scatter.6.cloned.1.call-update) | async-done | bytes 32784 | tf_op jit(solution)/shard_map/reduce_scatter | solution.py:130
  868.2 639.3 %reduce-scatter.10.cloned.1.call-done = f32[8,1024]{1,0:T(8,128)} async-done(((f32[1024,1024]{1,0:T(8,128)}), f32[8,1024]{1,0:T(8,128)}) %reduce-scatter.10.cloned.1.call-update) | async-done | bytes 32784
  1507.5 639.2 %reduce-scatter.8.cloned.1.call-done = f32[8,1024]{1,0:T(8,128)} async-done(((f32[1024,1024]{1,0:T(8,128)}), f32[8,1024]{1,0:T(8,128)}) %reduce-scatter.8.cloned.1.call-update) | async-done | bytes 32784 | tf_op jit(solution)/shard_map/reduce_scatter | solution.py:132
  (66 shorter events, 16.7 us)
Async XLA Ops:
  7.2 1.6 copy-start
  7.2 3.6 copy-start.6
  7.2 861.0 %reduce-scatter.6.cloned.1.call-start = ((), (), s32[]{:S(2)}) async-start(), calls=%async_computation.3 | async-start | bytes 4227072 | tf_op jit(solution)/shard_map/reduce_scatter | solution.py:130
  8.8 2.0 copy-start.4
  11.3 30.2 %copy-start.15 = (s32[1024,2]{0,1:T(2,128)S(1)}, s32[1024,2]{0,1:T(2,128)}, u32[]{:S(2)}) copy-start(s32[1024,2]{0,1:T(2,128)} %param.15) | copy-start | bytes 24580
  11.4 17.4 collective-permute-start
  15.4 17.2 collective-permute-start.1
  28.8 3.8 copy-start.9
  32.6 1.5 copy-start.10
  34.1 26.7 %collective-permute-start.2 = (bf16[3,1,320,1024]{3,2,1,0:T(8,128)(2,1)}, bf16[3,1,320,1024]{3,2,1,0:T(8,128)(2,1)}, u32[]{:S(2)}, u32[]{:S(2)}) collective-permute-start(bf16[3,1,320,1024]{3,2,1,0:T(8,128)(2,1)} %pad_maximum_fusion), channel_id=1, source_target_pairs={{0,1},{1,2},{2,3},{3,4},{4,5},{5,6},{6,7},{8,9},{9,10},{10,11},{11... | collective-permute-start | bytes 5898248 | tf_op jit(solution)/shard_map/ppermute | solution.py:15
  39.0 26.3 %collective-permute-start.3 = (bf16[3,1,320,1024]{3,2,1,0:T(8,128)(2,1)}, bf16[3,1,320,1024]{3,2,1,0:T(8,128)(2,1)}, u32[]{:S(2)}, u32[]{:S(2)}) collective-permute-start(bf16[3,1,320,1024]{3,2,1,0:T(8,128)(2,1)} %pad_maximum_fusion), channel_id=1, source_target_pairs={{1,0},{2,1},{3,2},{4,3},{5,4},{6,5},{7,6},{9,8},{10,9},{11,10},{12... | collective-permute-start | bytes 5898248 | tf_op jit(solution)/shard_map/ppermute | solution.py:17
  44.7 4.5 copy-start.11
  73.3 3.8 copy-start.14
  113.5 1.4 copy-start.1
  122.6 6.5 copy-start.2
  145.1 5.9 copy-start.12
  145.2 5.9 copy-start.16
  152.4 1.3 copy-start.13
  153.7 1353.8 %reduce-scatter.10.cloned.1.call-start = ((), (), s32[]{:S(2)}) async-start(), calls=%async_computation.5 | async-start | bytes 4227072
  153.8 2.9 copy-start.3
  157.2 85.2 %collective-permute-start.4 = (bf16[320,1024]{1,0:T(8,128)(2,1)S(1)}, bf16[320,1024]{1,0:T(8,128)(2,1)S(1)}, u32[]{:S(2)}, u32[]{:S(2)}) collective-permute-start(bf16[320,1024]{1,0:T(8,128)(2,1)S(1)} %get-tuple-element.306), channel_id=1, source_target_pairs={{0,8},{8,16},{16,24},{24,32},{32,40},{40,48},{48,56},{56,64},{64,7... | collective-permute-start | bytes 1966088 | tf_op jit(solution)/shard_map/ppermute | solution.py:27
  160.4 87.8 %collective-permute-start.5 = (bf16[320,1024]{1,0:T(8,128)(2,1)S(1)}, bf16[320,1024]{1,0:T(8,128)(2,1)S(1)}, u32[]{:S(2)}, u32[]{:S(2)}) collective-permute-start(bf16[320,1024]{1,0:T(8,128)(2,1)S(1)} %get-tuple-element.307), channel_id=1, source_target_pairs={{8,0},{16,8},{24,16},{32,24},{40,32},{48,40},{56,48},{64,56},{72,6... | collective-permute-start | bytes 1966088 | tf_op jit(solution)/shard_map/ppermute | solution.py:27
  161.7 86.6 %collective-permute-start.6 = (bf16[320,1024]{1,0:T(8,128)(2,1)S(1)}, bf16[320,1024]{1,0:T(8,128)(2,1)S(1)}, u32[]{:S(2)}, u32[]{:S(2)}) collective-permute-start(bf16[320,1024]{1,0:T(8,128)(2,1)S(1)} %get-tuple-element.309), channel_id=1, source_target_pairs={{0,1},{1,2},{2,3},{3,4},{4,5},{5,6},{6,7},{8,9},{9,10},{10,11},{11... | collective-permute-start | bytes 1966088 | tf_op jit(solution)/shard_map/ppermute | solution.py:27
  240.3 12.9 copy-start.7
  240.4 12.3 collective-permute-start.7
  261.4 1.0 copy-start.8
  261.5 1885.2 %reduce-scatter.8.cloned.1.call-start = ((), (), s32[]{:S(2)}) async-start(), calls=%async_computation.4 | async-start | bytes 4227072 | tf_op jit(solution)/shard_map/reduce_scatter | solution.py:132
  335.4 1.8 copy-start.5
Sparse Core Ops, SparseCore 0:
  153.8 714.3 reduce-scatter.5
  871.2 636.2 reduce-scatter.9
  1510.4 636.2 reduce-scatter.7
where the time goes:
time: 2160 us; the launch traced here: 2150 us
  waiting for transfers between devices  1850 us (86%)
  starting transfers between devices  97.5 us (5%)
  blocking collectives  70.3 us (3%)
  local copies, waits for them, and re-layouts  68.2 us (3%)
  matrix products  35.2 us (2%)
    unnamed x4, waiting for transfers between devices  639 us
    reduce_scatter x1, waiting for transfers between devices, body(): lax.psum_scatter(grad_out, ('region', 'sub'), scatter_dimension=0, tiled=...  639 us
    reduce_scatter x1, waiting for transfers between devices, body(): lax.psum_scatter(grad_src, ('region', 'sub'), scatter_dimension=0, tiled=...  529 us
    ppermute x4, starting transfers between devices, from_behind(): return lax.ppermute(block, axis, route)  85.2 us
    unnamed x1, blocking collectives  70.3 us
  transfers between devices with their start and end apart: 11, of which 9 were waited for; matrix products, arithmetic and copies ran while one was open for 1% of the time, Pallas kernels for 0%

commit v1 on v0

--- a/solution.py
+++ b/solution.py
@@ -1,7 +1,245 @@
 import jax
 import jax.numpy as jnp
 from jax import lax
+from jax.experimental import pallas as pl
+from jax.experimental.pallas import tpu as pltpu
 from jax.sharding import PartitionSpec as P
+
+MESH = pl.DeviceIdType.MESH
+ROUND = (0, 1, 2)
+ORDERS = ((0, 2, 1), (2, 1, 0), (1, 0, 2))
+BIAS_ORDER = (2, 1, 0)
+
+
+def device_at(coords, core):
+    return (coords[0] * 4 + coords[1], coords[2] * 2 + core)
+
+
+def moved(coords, dim, value):
+    return tuple(value if d == dim else c for d, c in enumerate(coords))
+
+
+def pick(blocks):
+    return tuple(blocks.get(d, slice(None)) for d in ROUND)
+
+
+def partner(half, position):
+    return position + 1 - 2 * (position % 2) if half == 0 else 3 - position
+
+
+def mesh_position():
+    region, sub = lax.axis_index("region"), lax.axis_index("sub")
+    return (region // 4, region % 4, sub // 2), sub % 2
+
+
+def reduce_kernel(
+    src_ref, dst_ref, out_ref, bias_ref, o_src, o_dst, o_out, o_bias,
+    acc, pair, r1, r2, r3, r4, fin, fin_r, b_acc, b_r,
+    load_sem, pair_s, pair_v, s1, v1, s2, v2, s3, v3, s4, v4, fin_s, fin_v, b_s, b_v,
+):
+    f32, bf16 = jnp.float32, jnp.bfloat16
+    mats, outs = (src_ref, dst_ref, out_ref), (o_src, o_dst, o_out)
+    coords, core = mesh_position()
+    mine = pl.ds(pl.multiple_of(core * 512, 512), 512)
+    theirs = pl.ds(pl.multiple_of((1 - core) * 512, 512), 512)
+    twin = device_at(coords, 1 - core)
+    ring = [
+        [device_at(moved(coords, dim, (coords[dim] + hop) % 4), core) for hop in (1, 2, 3)]
+        for dim in ROUND
+    ]
+    cols = (pl.ds(0, 256), pl.ds(256, 256))
+    sends = []
+
+    def remote(source, target, send, recv, device):
+        return pltpu.make_async_remote_copy(
+            src_ref=source, dst_ref=target, send_sem=send, recv_sem=recv,
+            device_id=device, device_id_type=MESH,
+        )
+
+    def go(copy):
+        copy.start()
+        sends.append(copy)
+        return copy
+
+    for m in range(3):
+        pltpu.make_async_copy(mats[m].at[:, :, :, :, mine], acc.at[m], load_sem.at[m]).start()
+    barrier = pltpu.get_barrier_semaphore()
+    peers = [twin] + ring[0] + ring[1] + ring[2]
+    for peer in peers:
+        pl.semaphore_signal(barrier, inc=1, device_id=peer, device_id_type=MESH)
+    pl.semaphore_wait(barrier, len(peers))
+
+    pairs = [
+        go(remote(mats[m].at[:, :, :, :, theirs], pair.at[m], pair_s.at[m], pair_v.at[m], twin))
+        for m in range(3)
+    ]
+
+    def step_one(m):
+        dim = ORDERS[m][0]
+        p = coords[dim]
+        copies = []
+        for half in range(2):
+            q = partner(half, p)
+            device = device_at(moved(coords, dim, q), core)
+            for slot, block in ((1, partner(1 - half, q)), (0, q)):
+                copies.append(go(remote(
+                    acc.at[(m, *pick({dim: block}), slice(None), cols[half])],
+                    r1.at[m, half, slot], s1.at[m, half, slot], v1.at[m, half, slot], device,
+                )))
+        return copies
+
+    def add_in(m, blocks, half, value_ref):
+        where = (m, *pick(blocks), slice(None), cols[half])
+        acc[where] = (acc[where].astype(f32) + value_ref[...].astype(f32)).astype(bf16)
+
+    def step_two(m, copies):
+        dim = ORDERS[m][0]
+        p = coords[dim]
+        started = []
+        for half in range(2):
+            copies[2 * half].wait_recv()
+            q = partner(1 - half, p)
+            add_in(m, {dim: q}, half, r1.at[m, half, 1])
+            started.append(go(remote(
+                acc.at[(m, *pick({dim: q}), slice(None), cols[half])],
+                r2.at[m, half], s2.at[m, half], v2.at[m, half],
+                device_at(moved(coords, dim, q), core),
+            )))
+        for half in range(2):
+            copies[2 * half + 1].wait_recv()
+            add_in(m, {dim: p}, half, r1.at[m, half, 0])
+        return started
+
+    def step_three(m, copies):
+        first, dim = ORDERS[m][0], ORDERS[m][1]
+        p = coords[first]
+        for half in range(2):
+            copies[half].wait_recv()
+            add_in(m, {first: p}, half, r2.at[m, half])
+        started = []
+        for hop in (2, 1, 3):
+            block = (coords[dim] + hop) % 4
+            started.append(go(remote(
+                acc.at[(m, *pick({first: p, dim: block}))],
+                r3.at[m, hop - 1], s3.at[m, hop - 1], v3.at[m, hop - 1], ring[dim][hop - 1],
+            )))
+        return started
+
+    def step_four(m, copies):
+        first, second, dim = ORDERS[m]
+        for copy in copies:
+            copy.wait_recv()
+        where = (m, *pick({first: coords[first], second: coords[second]}))
+        total = acc[where].astype(f32)
+        for slot in range(3):
+            total = total + r3[m, slot].astype(f32)
+        acc[where] = total.astype(bf16)
+        started = []
+        for hop in (2, 1, 3):
+            block = (coords[dim] + hop) % 4
+            started.append(go(remote(
+                acc.at[(m, *pick({first: coords[first], second: coords[second], dim: block}))],
+                r4.at[m, hop - 1], s4.at[m, hop - 1], v4.at[m, hop - 1], ring[dim][hop - 1],
+            )))
+        return started
+
+    def step_five(m, copies):
+        for copy in copies:
+            copy.wait_recv()
+        total = acc[(m, *coords)].astype(f32)
+        for slot in range(3):
+            total = total + r4[m, slot].astype(f32)
+        fin[m, 0] = total[:8]
+        fin[m, 1] = total[8:]
+        return go(remote(fin.at[m, 1 - core], fin_r.at[m], fin_s.at[m], fin_v.at[m], twin))
+
+    def bias_send(stage):
+        if stage == 3:
+            return [go(remote(b_acc.at[3], b_r.at[9], b_s.at[9], b_v.at[9], twin))]
+        started = []
+        for hop in range(3):
+            slot = 3 * stage + hop
+            started.append(go(remote(
+                b_acc.at[stage], b_r.at[slot], b_s.at[slot], b_v.at[slot],
+                ring[BIAS_ORDER[stage]][hop],
+            )))
+        return started
+
+    def bias_add(stage, copies):
+        total = b_acc[stage]
+        for copy in copies:
+            copy.wait_recv()
+        for slot in range(3 * stage, 3 * stage + len(copies)):
+            total = total + b_r[slot]
+        return total
+
+    b_acc[0] = bias_ref[...]
+    b_copies = bias_send(0)
+    state = []
+    for m in range(3):
+        pltpu.make_async_copy(mats[m].at[:, :, :, :, mine], acc.at[m], load_sem.at[m]).wait()
+        pairs[m].wait_recv()
+
+        def add_rows(i, carry, m=m):
+            z, y = i // 4, i % 4
+            acc[m, z, y] = (acc[m, z, y].astype(f32) + pair[m, z, y].astype(f32)).astype(bf16)
+            return carry
+
+        lax.fori_loop(0, 16, add_rows, 0)
+        state.append(step_one(m))
+    b_acc[1] = bias_add(0, b_copies)
+    b_copies = bias_send(1)
+    state = [step_two(m, state[m]) for m in range(3)]
+    b_acc[2] = bias_add(1, b_copies)
+    b_copies = bias_send(2)
+    state = [step_three(m, state[m]) for m in range(3)]
+    b_acc[3] = bias_add(2, b_copies)
+    b_copies = bias_send(3)
+    state = [step_four(m, state[m]) for m in range(3)]
+    state = [step_five(m, state[m]) for m in range(3)]
+    o_bias[...] = bias_add(3, b_copies)
+    for m in range(3):
+        state[m].wait_recv()
+        outs[m][:, mine] = fin[m, core]
+        outs[m][:, theirs] = fin_r[m]
+    for copy in sends:
+        copy.wait_send()
+
+
+def reduce_scatter(src, dst, out, bias):
+    f32, bf16 = jnp.float32, jnp.bfloat16
+    dma = pltpu.SemaphoreType.DMA
+    vmem = pl.BlockSpec(memory_space=pltpu.VMEM)
+    hbm = pl.BlockSpec(memory_space=pl.ANY)
+    view = (4, 4, 4, 16, 1024)
+    slab = jax.ShapeDtypeStruct((8, 1024), f32)
+    o_src, o_dst, o_out, o_bias = pl.pallas_call(
+        reduce_kernel,
+        out_shape=(slab, slab, slab, jax.ShapeDtypeStruct((8, 128), f32)),
+        in_specs=[hbm, hbm, hbm, vmem],
+        out_specs=[vmem] * 4,
+        scratch_shapes=[
+            pltpu.VMEM((3, 4, 4, 4, 16, 512), bf16),
+            pltpu.VMEM((3, 4, 4, 4, 16, 512), bf16),
+            pltpu.VMEM((3, 2, 2, 4, 4, 16, 256), bf16),
+            pltpu.VMEM((3, 2, 4, 4, 16, 256), bf16),
+            pltpu.VMEM((3, 3, 4, 16, 512), bf16),
+            pltpu.VMEM((3, 3, 16, 512), bf16),
+            pltpu.VMEM((3, 2, 8, 512), f32),
+            pltpu.VMEM((3, 8, 512), f32),
+            pltpu.VMEM((4, 8, 128), f32),
+            pltpu.VMEM((10, 8, 128), f32),
+            dma((3,)), dma((3,)), dma((3,)), dma((3, 2, 2)), dma((3, 2, 2)), dma((3, 2)), dma((3, 2)),
+            dma((3, 3)), dma((3, 3)), dma((3, 3)), dma((3, 3)), dma((3,)), dma((3,)), dma((10,)), dma((10,)),
+        ],
+        compiler_params=pltpu.CompilerParams(
+            collective_id=1, has_side_effects=True, vmem_limit_bytes=32 * 1024 * 1024
+        ),
+        name="reduce_scatter",
+    )(src.reshape(view), dst.reshape(view), out.reshape(view), bias.reshape(8, 128))
+    index = lax.axis_index("region") * 8 + lax.axis_index("sub")
+    part_bias = lax.dynamic_slice(o_bias.reshape(1024), (index * 8,), (8,))
+    return o_src, o_dst, o_out, part_bias
 
 
 def with_halo(cells, sides, width):
@@ -126,11 +364,8 @@
     node_grad = (cotangent.astype(f32) + contract_cols(node_back, w_dst)).astype(bf16)
     grad_dst = contract_rows(nodes, node_back)
     grad_out = contract_rows(node_sum, cotangent)
-    part_src, part_dst, part_out, part_bias = (
-        lax.psum_scatter(grad_src, ("region", "sub"), scatter_dimension=0, tiled=True),
-        lax.psum_scatter(grad_dst, ("region", "sub"), scatter_dimension=0, tiled=True),
-        lax.psum_scatter(grad_out, ("region", "sub"), scatter_dimension=0, tiled=True),
-        lax.psum_scatter(grad_bias, ("region", "sub"), scatter_dimension=0, tiled=True),
+    part_src, part_dst, part_out, part_bias = reduce_scatter(
+        grad_src.astype(bf16), grad_dst.astype(bf16), grad_out.astype(bf16), grad_bias
     )
     return (updated, token_grad, node_grad, part_src, part_dst, part_out, part_bias)
 

time: 2160 us -> 287 us (0.13)
  waiting for transfers between devices: 1850 us -> 34 us
  starting transfers between devices: 97.5 us -> 24 us
  blocking collectives: 70.3 us -> 0 us
  Pallas kernels: 0 us -> 45.4 us
  local copies, waits for them, and re-layouts: 68.2 us -> 113 us
    reduce_scatter x2 -> x0, waiting for transfers between devices: 1170 us -> none  [the longest x1 639 us: body(): lax.psum_scatter(grad_out, ('region', 'sub'), scatter_dimension=0, tiled=...]
    unnamed x4 -> x0, waiting for transfers between devices: 639 us -> none
    ppermute x4, starting transfers between devices: 85.2 us -> 11 us  [from_behind(): return lax.ppermute(block, axis, route)]
    unnamed x1 -> x0, blocking collectives: 70.3 us -> none
    pallas_call x0 -> x1, Pallas kernels: none -> 45.4 us  [reduce_scatter(): pl.pallas_call(reduce_kernel, out_shape=(slab, slab, slab, jax.ShapeDtype...]
  transfers between devices with their start and end apart: 11 -> 8, of which waited for: 9 -> 7; matrix products, arithmetic and copies ran while one was open for 1% -> 4% of each run, Pallas kernels for 0% -> 0%
where the time goes in v1:
time: 287 us; the launch traced here: 285 us
  local copies, waits for them, and re-layouts  113 us (39%)
  Pallas kernels  45.4 us (16%)
  matrix products  36.7 us (13%)
  waiting for transfers between devices  34 us (12%)
  other arithmetic  30.5 us (11%)
  starting transfers between devices  24 us (8%)
    pallas_call x1, Pallas kernels, reduce_scatter(): pl.pallas_call(reduce_kernel, out_shape=(slab, slab, slab, jax.ShapeDtype...  45.4 us
    gather x4, local copies, waits for them, and re-layouts, one_block(): upstream = jnp.take(near_up, near_block, axis=0).astype(f32)  23.6 us
    gather x4, local copies, waits for them, and re-layouts, one_block(): jnp.take(near_proj, near_block, axis=0).astype(f32)  23.6 us
    dot_general x8, matrix products, contract_rows(): lax.dot_general(left, right, (((0,), (0,)), ((), ())), preferred_element_...  22.3 us
    ppermute x2, waiting for transfers between devices, with_halo(): lax.ppermute(head, axis, [((i + 1) % count, i) for i in range(ends)])  15.3 us
    ppermute x2, waiting for transfers between devices, with_halo(): lax.ppermute(tail, axis, [(i, (i + 1) % count) for i in range(ends)])  13.6 us
    ppermute x4, starting transfers between devices, from_behind(): return lax.ppermute(block, axis, route)  11 us
    convert_element_type x2, local copies, waits for them, and re-layouts, one_block(): (upstream * sigma * (1.0 + preact * (1.0 - sigma)) * live_mask).astype(bf16)  10.1 us
  transfers between devices with their start and end apart: 8, of which 7 were waited for; matrix products, arithmetic and copies ran while one was open for 4% of the time, Pallas kernels for 0%

profile of v1, /device:TPU:1, one launch (start us, length us, event | category | flops | bytes accessed | tf_op | source)
XLA Modules:
  0.0 285.4 jit_solution(8981606270466456079)
XLA Ops:
  5.9 4.7 %collective-permute-start = (bf16[1,1,320,1024]{3,2,1,0:T(8,128)(2,1)S(1)}, bf16[1,1,320,1024]{3,2,1,0:T(8,128)(2,1)S(1)}, u32[]{:S(2)}, u32[]{:S(2)}) collective-permute-start(bf16[1,1,320,1024]{3,2,1,0:T(8,128)(2,1)S(1)} %fusion.38), channel_id=1, source_target_pairs={{0,8},{8,16},{16,24},{24,32},{32,40},{40,48},{48,56},{56,64},{64,7... | collective-permute-start | bytes 1966088 | tf_op jit(solution)/shard_map/ppermute | solution.py:253
  10.7 12.1 %collective-permute-done.1 = bf16[1,1,320,1024]{3,2,1,0:T(8,128)(2,1)S(1)} collective-permute-done((bf16[1,1,320,1024]{3,2,1,0:T(8,128)(2,1)S(1)}, bf16[1,1,320,1024]{3,2,1,0:T(8,128)(2,1)S(1)}, u32[]{:S(2)}, u32[]{:S(2)}) %collective-permute-start.1) | collective-permute-done | bytes 655392 | tf_op jit(solution)/shard_map/ppermute | solution.py:255
  25.9 5.1 %collective-permute-start.2 = (bf16[3,1,320,1024]{3,2,1,0:T(8,128)(2,1)}, bf16[3,1,320,1024]{3,2,1,0:T(8,128)(2,1)}, u32[]{:S(2)}, u32[]{:S(2)}) collective-permute-start(bf16[3,1,320,1024]{3,2,1,0:T(8,128)(2,1)} %pad_maximum_fusion), channel_id=1, source_target_pairs={{0,1},{1,2},{2,3},{3,4},{4,5},{5,6},{6,7},{8,9},{9,10},{10,11},{11... | collective-permute-start | bytes 5898248 | tf_op jit(solution)/shard_map/ppermute | solution.py:253
  31.0 1.9 collective-permute-start.3
  36.8 3.3 %fusion.34 = s32[1024,2]{1,0:T(8,128)} fusion(s32[1024,2]{1,0:T(8,128)} %copy.46, s32[1024,2]{1,0:T(8,128)} %copy.47, s32[1024,2]{1,0:T(8,128)} %copy.42, s32[]{:T(128)S(6)} %axis_index.33, s32[]{:T(128)S(6)} %axis_index.15), kind=kLoop, calls=%fused_computation.79 | loop fusion | flops 83968 | bytes 32776 | tf_op jit(solution)/shard_map/add | solution.py:308
  40.2 12.7 %collective-permute-done.2 = bf16[3,1,320,1024]{3,2,1,0:T(8,128)(2,1)} collective-permute-done((bf16[3,1,320,1024]{3,2,1,0:T(8,128)(2,1)}, bf16[3,1,320,1024]{3,2,1,0:T(8,128)(2,1)}, u32[]{:S(2)}, u32[]{:S(2)}) %collective-permute-start.2) | collective-permute-done | bytes 1966112 | tf_op jit(solution)/shard_map/ppermute | solution.py:253
  54.0 3.3 %collective-permute-done.3 = bf16[3,1,320,1024]{3,2,1,0:T(8,128)(2,1)} collective-permute-done((bf16[3,1,320,1024]{3,2,1,0:T(8,128)(2,1)}, bf16[3,1,320,1024]{3,2,1,0:T(8,128)(2,1)}, u32[]{:S(2)}, u32[]{:S(2)}) %collective-permute-start.3) | collective-permute-done | bytes 1966112 | tf_op jit(solution)/shard_map/ppermute | solution.py:255
  58.4 2.2 fusion.43
  62.3 2.2 broadcast.45.clone
  64.5 2.1 broadcast.45
  66.6 2.5 broadcast_in_dim.34
  69.1 138.1 %while.21 = (s32[]{:T(128)}, f32[800,1024]{1,0:T(8,128)}, f32[800,1024]{1,0:T(8,128)}, f32[1024,1024]{1,0:T(8,128)}, f32[1024]{0:T(1024)S(1)}, /*index=5*/bf16[1...) while((s32[]{:T(128)}, f32[800,1024]{1,0:T(8,128)}, ...), condition=%wide.region_3.5_spmd.clone, body=%wide.region_0.4_spmd.clone.sunk | while | flops 6604074496 | bytes 202986064 | solution.py:344
  71.3 7.7 %gather_fusion.1 = bf16[1024,1024]{1,0:T(8,128)(2,1)} fusion(bf16[800,1024]{1,0:T(8,128)(2,1)} %get-tuple-element.432, s32[1024]{0:T(1024)S(1)} %broadcast_clamp_fusion.2), kind=kCustom, calls=%fused_computation.1.clone.clone.1 | custom fusion | bytes 4198400 | tf_op jit(solution)/shard_map/while/body/jit(_take)/gather | solution.py:324
  78.9 4.1 %reshape.130 = bf16[512,2,1024]{2,1,0:T(2,128)(2,1)} reshape(bf16[1024,1024]{1,0:T(8,128)(2,1)} %gather_fusion.1) | data formatting | bytes 4194304 | tf_op jit(solution)/shard_map/while/body/jit(_take)/gather | solution.py:324
  83.1 7.7 %gather_fusion = bf16[1024,1024]{1,0:T(8,128)(2,1)} fusion(bf16[800,1024]{1,0:T(8,128)(2,1)} %get-tuple-element.429, s32[1024]{0:T(1024)S(1)} %broadcast_clamp_fusion.2), kind=kCustom, calls=%fused_computation.clone.clone.1 | custom fusion | bytes 4198400 | tf_op jit(solution)/shard_map/while/body/jit(_take)/gather | solution.py:321
  90.8 4.1 %reshape.129 = bf16[512,2,1024]{2,1,0:T(2,128)(2,1)} reshape(bf16[1024,1024]{1,0:T(8,128)(2,1)} %gather_fusion) | data formatting | bytes 4194304 | tf_op jit(solution)/shard_map/while/body/jit(_take)/gather | solution.py:321
  94.9 3.3 %fusion.80 = f32[512,1024]{1,0:T(8,128)S(1)} fusion(bf16[1024,1024]{1,0:T(8,128)(2,1)} %get-tuple-element.428, bf16[1024,1024]{1,0:T(8,128)(2,1)} %get-tuple-element.427, s32[]{:T(128)S(6)} %select_n.110), kind=kOutput, calls=%fused_computation.21.clone.1 | convolution fusion | flops 1073741824 | bytes 5242884 | tf_op jit(solution)/shard_map/while/body/dot_general | solution.py:320
  98.2 4.5 %convert_reduce_fusion.2 = (f32[1024]{0:T(1024)S(1)}, bf16[512,2,1024]{2,0,1:T(8,128)(2,1)}, bf16[512,2,1024]{2,0,1:T(8,128)(2,1)S(1)}) fusion(f32[512]{0:T(512)S(1)} %fusion.79, f32[1024]{0:T(1024)S(1)} %get-tuple-element.430, bf16[512,2,1024]{2,1,0:T(2,128)(2,1)S(1)} %copy-done.4, f32[512,1024]{1,0:T(8,128)S(1)} %fusion.80, ...), kind=kLoop, calls=%fused_computation.3.clone.1 | loop fusion | flops 22019072 | bytes 10497024 | tf_op jit(solution)/shard_map/while/body/reduce_sum | solution.py:334
  102.7 3.4 %copy.63 = bf16[512,2,1024]{2,1,0:T(2,128)(2,1)} copy(bf16[512,2,1024]{2,0,1:T(8,128)(2,1)S(1)} %get-tuple-element.378) | data formatting | bytes 4194304 | tf_op jit(solution)/shard_map/while/body/convert_element_type | solution.py:323
  106.2 4.1 %reshape.131 = bf16[1024,1024]{1,0:T(8,128)(2,1)} reshape(bf16[512,2,1024]{2,1,0:T(2,128)(2,1)} %copy.63) | data formatting | bytes 4194304 | tf_op jit(solution)/shard_map/while/body/reshape | solution.py:327
  110.3 2.2 reduce_sum.30
  112.5 5.0 %copy.64 = bf16[512,2,1024]{2,1,0:T(2,128)(2,1)} copy(bf16[512,2,1024]{2,0,1:T(8,128)(2,1)} %get-tuple-element.379) | data formatting | bytes 4194304 | tf_op jit(solution)/shard_map/while/body/convert_element_type | solution.py:325
  117.5 4.1 %reshape.132 = bf16[1024,1024]{1,0:T(8,128)(2,1)} reshape(bf16[512,2,1024]{2,1,0:T(2,128)(2,1)} %copy.64) | data formatting | bytes 4194304 | tf_op jit(solution)/shard_map/while/body/reshape | solution.py:328
  121.6 6.5 %fusion.82 = f32[800,1024]{1,0:T(8,128)} fusion(f32[800,1024]{1,0:T(8,128)} %get-tuple-element.402, bf16[1024,1024]{1,0:T(8,128)(2,1)} %reshape.132, s32[1024]{0:T(1024)S(1)} %eq.82), kind=kOutput, calls=%fused_computation.17.clone.1 | convolution fusion | flops 1679360000 | bytes 8654848 | tf_op jit(solution)/shard_map/while/body/dot_general | solution.py:269
  128.2 2.4 fusion.81
  136.1 2.0 copy-done.2
  140.3 7.7 %gather_fusion.1 = bf16[1024,1024]{1,0:T(8,128)(2,1)} fusion(bf16[800,1024]{1,0:T(8,128)(2,1)} %get-tuple-element.432, s32[1024]{0:T(1024)S(1)} %broadcast_clamp_fusion.2), kind=kCustom, calls=%fused_computation.1.clone.clone.1 | custom fusion | bytes 4198400 | tf_op jit(solution)/shard_map/while/body/jit(_take)/gather | solution.py:324
  148.0 4.1 %reshape.130 = bf16[512,2,1024]{2,1,0:T(2,128)(2,1)} reshape(bf16[1024,1024]{1,0:T(8,128)(2,1)} %gather_fusion.1) | data formatting | bytes 4194304 | tf_op jit(solution)/shard_map/while/body/jit(_take)/gather | solution.py:324
  152.1 7.7 %gather_fusion = bf16[1024,1024]{1,0:T(8,128)(2,1)} fusion(bf16[800,1024]{1,0:T(8,128)(2,1)} %get-tuple-element.429, s32[1024]{0:T(1024)S(1)} %broadcast_clamp_fusion.2), kind=kCustom, calls=%fused_computation.clone.clone.1 | custom fusion | bytes 4198400 | tf_op jit(solution)/shard_map/while/body/jit(_take)/gather | solution.py:321
  159.8 4.1 %reshape.129 = bf16[512,2,1024]{2,1,0:T(2,128)(2,1)} reshape(bf16[1024,1024]{1,0:T(8,128)(2,1)} %gather_fusion) | data formatting | bytes 4194304 | tf_op jit(solution)/shard_map/while/body/jit(_take)/gather | solution.py:321
  163.9 3.3 %fusion.80 = f32[512,1024]{1,0:T(8,128)S(1)} fusion(bf16[1024,1024]{1,0:T(8,128)(2,1)} %get-tuple-element.428, bf16[1024,1024]{1,0:T(8,128)(2,1)} %get-tuple-element.427, s32[]{:T(128)S(6)} %select_n.110), kind=kOutput, calls=%fused_computation.21.clone.1 | convolution fusion | flops 1073741824 | bytes 5242884 | tf_op jit(solution)/shard_map/while/body/dot_general | solution.py:320
  167.2 4.5 %convert_reduce_fusion.2 = (f32[1024]{0:T(1024)S(1)}, bf16[512,2,1024]{2,0,1:T(8,128)(2,1)}, bf16[512,2,1024]{2,0,1:T(8,128)(2,1)S(1)}) fusion(f32[512]{0:T(512)S(1)} %fusion.79, f32[1024]{0:T(1024)S(1)} %get-tuple-element.430, bf16[512,2,1024]{2,1,0:T(2,128)(2,1)S(1)} %copy-done.4, f32[512,1024]{1,0:T(8,128)S(1)} %fusion.80, ...), kind=kLoop, calls=%fused_computation.3.clone.1 | loop fusion | flops 22019072 | bytes 10497024 | tf_op jit(solution)/shard_map/while/body/reduce_sum | solution.py:334
  171.8 3.4 %copy.63 = bf16[512,2,1024]{2,1,0:T(2,128)(2,1)} copy(bf16[512,2,1024]{2,0,1:T(8,128)(2,1)S(1)} %get-tuple-element.378) | data formatting | bytes 4194304 | tf_op jit(solution)/shard_map/while/body/convert_element_type | solution.py:323
  175.2 4.1 %reshape.131 = bf16[1024,1024]{1,0:T(8,128)(2,1)} reshape(bf16[512,2,1024]{2,1,0:T(2,128)(2,1)} %copy.63) | data formatting | bytes 4194304 | tf_op jit(solution)/shard_map/while/body/reshape | solution.py:327
  179.4 2.2 reduce_sum.30
  181.5 5.0 %copy.64 = bf16[512,2,1024]{2,1,0:T(2,128)(2,1)} copy(bf16[512,2,1024]{2,0,1:T(8,128)(2,1)} %get-tuple-element.379) | data formatting | bytes 4194304 | tf_op jit(solution)/shard_map/while/body/convert_element_type | solution.py:325
  186.6 4.1 %reshape.132 = bf16[1024,1024]{1,0:T(8,128)(2,1)} reshape(bf16[512,2,1024]{2,1,0:T(2,128)(2,1)} %copy.64) | data formatting | bytes 4194304 | tf_op jit(solution)/shard_map/while/body/reshape | solution.py:328
  190.7 6.5 %fusion.82 = f32[800,1024]{1,0:T(8,128)} fusion(f32[800,1024]{1,0:T(8,128)} %get-tuple-element.402, bf16[1024,1024]{1,0:T(8,128)(2,1)} %reshape.132, s32[1024]{0:T(1024)S(1)} %eq.82), kind=kOutput, calls=%fused_computation.17.clone.1 | convolution fusion | flops 1679360000 | bytes 8654848 | tf_op jit(solution)/shard_map/while/body/dot_general | solution.py:269
  197.2 2.4 fusion.81
  205.2 2.0 copy-done.2
  207.1 2.3 convert_element_type.107
  212.3 4.1 %collective-permute-start.4 = (bf16[320,1024]{1,0:T(8,128)(2,1)}, bf16[320,1024]{1,0:T(8,128)(2,1)S(1)}, u32[]{:S(2)}, u32[]{:S(2)}) collective-permute-start(bf16[320,1024]{1,0:T(8,128)(2,1)} %get-tuple-element.279), channel_id=1, source_target_pairs={{0,8},{8,16},{16,24},{24,32},{32,40},{40,48},{48,56},{56,64},{64,7... | collective-permute-start | bytes 1966088 | tf_op jit(solution)/shard_map/ppermute | solution.py:265
  219.7 3.6 %collective-permute-start.6 = (bf16[320,1024]{1,0:T(8,128)(2,1)}, bf16[320,1024]{1,0:T(8,128)(2,1)}, u32[]{:S(2)}, u32[]{:S(2)}) collective-permute-start(bf16[320,1024]{1,0:T(8,128)(2,1)} %get-tuple-element.282), channel_id=1, source_target_pairs={{0,1},{1,2},{2,3},{3,4},{4,5},{5,6},{6,7},{8,9},{9,10},{10,11},{11... | collective-permute-start | bytes 1966088 | tf_op jit(solution)/shard_map/ppermute | solution.py:265
  223.4 2.7 convert_element_type.118
  226.1 1.9 collective-permute-done.5
  228.0 2.0 collective-permute-done.7
  231.2 1.9 fusion.18
  237.6 45.4 %reduce_scatter.1 = (f32[8,1024]{1,0:T(8,128)S(1)}, f32[8,1024]{1,0:T(8,128)S(1)}, f32[8,1024]{1,0:T(8,128)S(1)}, f32[8,128]{1,0:T(8,128)S(1)}) custom-call(bf16[4,4,4,16,1024]{4,3,2,1,0:T(8,128)(2,1)S(1)} %bitcast.68, bf16[4,4,4,16,1024]{4,3,2,1,0:T(8,128)(2,1)S(1)} %bitcast.70, bf16[4,4,4,16,1024]{4,3,2,1,0:T(8,128)(2,1)S(1)} %bitcast.69, ...), custom_call_target="tpu_custom_call" | custom-call | tf_op jit(solution)/shard_map/reduce_scatter/pallas_call | solution.py:216
  (123 shorter events, 45.0 us)
Async XLA Ops:
  0.6 1.6 copy-start
  0.6 3.1 %copy-start.16 = (bf16[160,1024]{1,0:T(8,128)(2,1)S(1)}, bf16[160,1024]{1,0:T(8,128)(2,1)}, u32[]{:S(2)}) copy-start(bf16[160,1024]{1,0:T(8,128)(2,1)} %param.21) | copy-start | bytes 983044
  0.7 3.1 %copy-start.14 = (bf16[1024,1024]{1,0:T(8,128)(2,1)S(1)}, bf16[1024,1024]{1,0:T(8,128)(2,1)}, u32[]{:S(2)}) copy-start(bf16[1024,1024]{1,0:T(8,128)(2,1)} %param.20) | copy-start | bytes 6291460
  4.6 29.0 %copy-start.24 = (s32[1024,2]{0,1:T(2,128)S(1)}, s32[1024,2]{0,1:T(2,128)}, u32[]{:S(2)}) copy-start(s32[1024,2]{0,1:T(2,128)} %param.15) | copy-start | bytes 24580
  4.6 18.1 %collective-permute-start.1 = (bf16[1,1,320,1024]{3,2,1,0:T(8,128)(2,1)S(1)}, bf16[1,1,320,1024]{3,2,1,0:T(8,128)(2,1)S(1)}, u32[]{:S(2)}, u32[]{:S(2)}) collective-permute-start(bf16[1,1,320,1024]{3,2,1,0:T(8,128)(2,1)S(1)} %fusion.38), channel_id=1, source_target_pairs={{8,0},{16,8},{24,16},{32,24},{40,32},{48,40},{56,48},{64,56},{72,6... | collective-permute-start | bytes 1966088 | tf_op jit(solution)/shard_map/ppermute | solution.py:255
  5.9 17.6 %collective-permute-start = (bf16[1,1,320,1024]{3,2,1,0:T(8,128)(2,1)S(1)}, bf16[1,1,320,1024]{3,2,1,0:T(8,128)(2,1)S(1)}, u32[]{:S(2)}, u32[]{:S(2)}) collective-permute-start(bf16[1,1,320,1024]{3,2,1,0:T(8,128)(2,1)S(1)} %fusion.38), channel_id=1, source_target_pairs={{0,8},{8,16},{16,24},{24,32},{32,40},{40,48},{48,56},{56,64},{64,7... | collective-permute-start | bytes 1966088 | tf_op jit(solution)/shard_map/ppermute | solution.py:253
  23.6 0.8 copy-start.19
  25.9 27.0 %collective-permute-start.2 = (bf16[3,1,320,1024]{3,2,1,0:T(8,128)(2,1)}, bf16[3,1,320,1024]{3,2,1,0:T(8,128)(2,1)}, u32[]{:S(2)}, u32[]{:S(2)}) collective-permute-start(bf16[3,1,320,1024]{3,2,1,0:T(8,128)(2,1)} %pad_maximum_fusion), channel_id=1, source_target_pairs={{0,1},{1,2},{2,3},{3,4},{4,5},{5,6},{6,7},{8,9},{9,10},{10,11},{11... | collective-permute-start | bytes 5898248 | tf_op jit(solution)/shard_map/ppermute | solution.py:253
  31.0 26.3 %collective-permute-start.3 = (bf16[3,1,320,1024]{3,2,1,0:T(8,128)(2,1)}, bf16[3,1,320,1024]{3,2,1,0:T(8,128)(2,1)}, u32[]{:S(2)}, u32[]{:S(2)}) collective-permute-start(bf16[3,1,320,1024]{3,2,1,0:T(8,128)(2,1)} %pad_maximum_fusion), channel_id=1, source_target_pairs={{1,0},{2,1},{3,2},{4,3},{5,4},{6,5},{7,6},{9,8},{10,9},{11,10},{12... | collective-permute-start | bytes 5898248 | tf_op jit(solution)/shard_map/ppermute | solution.py:255
  36.7 3.3 %copy-start.20 = (bf16[1,1,320,1024]{3,2,1,0:T(8,128)(2,1)S(1)}, bf16[1,1,320,1024]{3,2,1,0:T(8,128)(2,1)}, u32[]{:S(2)}) copy-start(bf16[1,1,320,1024]{3,2,1,0:T(8,128)(2,1)} %copy-done.19) | copy-start | bytes 1966084
  66.6 2.5 copy-start.23
  94.9 3.3 %copy-start.3 = (bf16[512,2,1024]{2,1,0:T(2,128)(2,1)S(1)}, bf16[512,2,1024]{2,1,0:T(2,128)(2,1)}, u32[]{:S(2)}) copy-start(bf16[512,2,1024]{2,1,0:T(2,128)(2,1)} %reshape.130) | copy-start | bytes 6291460 | tf_op jit(solution)/shard_map/while
  94.9 3.3 %copy-start.4 = (bf16[512,2,1024]{2,1,0:T(2,128)(2,1)S(1)}, bf16[512,2,1024]{2,1,0:T(2,128)(2,1)}, u32[]{:S(2)}) copy-start(bf16[512,2,1024]{2,1,0:T(2,128)(2,1)} %reshape.129) | copy-start | bytes 6291460 | tf_op jit(solution)/shard_map/while
  121.6 6.5 %copy-start.5 = (bf16[1024,1024]{1,0:T(8,128)(2,1)S(1)}, bf16[1024,1024]{1,0:T(8,128)(2,1)}, u32[]{:S(2)}) copy-start(bf16[1024,1024]{1,0:T(8,128)(2,1)} %reshape.131) | copy-start | bytes 6291460 | tf_op jit(solution)/shard_map/while
  121.6 6.5 %copy-start.12 = (f32[800,1024]{1,0:T(8,128)S(1)}, f32[800,1024]{1,0:T(8,128)}, u32[]{:S(2)}) copy-start(f32[800,1024]{1,0:T(8,128)} %get-tuple-element.401) | copy-start | bytes 9830404 | tf_op jit(solution)/shard_map/while
  128.1 2.5 copy-start.21
  128.1 2.5 copy-start.25
  130.6 1.7 copy-start.13
  130.6 3.4 %copy-start.1 = (f32[1024,1024]{1,0:T(8,128)S(1)}, f32[1024,1024]{1,0:T(8,128)}, u32[]{:S(2)}) copy-start(f32[1024,1024]{1,0:T(8,128)} %get-tuple-element.403) | copy-start | bytes 12582916 | tf_op jit(solution)/shard_map/while
  130.6 4.0 %copy-start.10 = (bf16[1024,1024]{1,0:T(8,128)(2,1)S(1)}, bf16[1024,1024]{1,0:T(8,128)(2,1)}, u32[]{:S(2)}) copy-start(bf16[1024,1024]{1,0:T(8,128)(2,1)} %get-tuple-element.427) | copy-start | bytes 6291460 | tf_op jit(solution)/shard_map/while
  134.7 1.5 copy-start.22
  136.1 2.0 copy-start.2
  163.9 3.3 %copy-start.3 = (bf16[512,2,1024]{2,1,0:T(2,128)(2,1)S(1)}, bf16[512,2,1024]{2,1,0:T(2,128)(2,1)}, u32[]{:S(2)}) copy-start(bf16[512,2,1024]{2,1,0:T(2,128)(2,1)} %reshape.130) | copy-start | bytes 6291460 | tf_op jit(solution)/shard_map/while
  163.9 3.3 %copy-start.4 = (bf16[512,2,1024]{2,1,0:T(2,128)(2,1)S(1)}, bf16[512,2,1024]{2,1,0:T(2,128)(2,1)}, u32[]{:S(2)}) copy-start(bf16[512,2,1024]{2,1,0:T(2,128)(2,1)} %reshape.129) | copy-start | bytes 6291460 | tf_op jit(solution)/shard_map/while
  190.7 6.5 %copy-start.5 = (bf16[1024,1024]{1,0:T(8,128)(2,1)S(1)}, bf16[1024,1024]{1,0:T(8,128)(2,1)}, u32[]{:S(2)}) copy-start(bf16[1024,1024]{1,0:T(8,128)(2,1)} %reshape.131) | copy-start | bytes 6291460 | tf_op jit(solution)/shard_map/while
  190.7 6.5 %copy-start.12 = (f32[800,1024]{1,0:T(8,128)S(1)}, f32[800,1024]{1,0:T(8,128)}, u32[]{:S(2)}) copy-start(f32[800,1024]{1,0:T(8,128)} %get-tuple-element.401) | copy-start | bytes 9830404 | tf_op jit(solution)/shard_map/while
  197.2 2.5 copy-start.21
  197.2 2.5 copy-start.25
  199.6 1.7 copy-start.13
  199.7 3.4 %copy-start.1 = (f32[1024,1024]{1,0:T(8,128)S(1)}, f32[1024,1024]{1,0:T(8,128)}, u32[]{:S(2)}) copy-start(f32[1024,1024]{1,0:T(8,128)} %get-tuple-element.403) | copy-start | bytes 12582916 | tf_op jit(solution)/shard_map/while
  199.7 4.0 %copy-start.10 = (bf16[1024,1024]{1,0:T(8,128)(2,1)S(1)}, bf16[1024,1024]{1,0:T(8,128)(2,1)}, u32[]{:S(2)}) copy-start(bf16[1024,1024]{1,0:T(8,128)(2,1)} %get-tuple-element.427) | copy-start | bytes 6291460 | tf_op jit(solution)/shard_map/while
  203.7 1.5 copy-start.22
  205.2 2.0 copy-start.2
  207.1 2.9 %copy-start.11 = (f32[800,1024]{1,0:T(8,128)S(1)}, f32[800,1024]{1,0:T(8,128)}, u32[]{:S(2)}) copy-start(f32[800,1024]{1,0:T(8,128)} %get-tuple-element.205) | copy-start | bytes 9830404
  209.5 1.2 copy-start.6
  210.3 2.0 copy-start.8
  212.3 13.7 %collective-permute-start.4 = (bf16[320,1024]{1,0:T(8,128)(2,1)}, bf16[320,1024]{1,0:T(8,128)(2,1)S(1)}, u32[]{:S(2)}, u32[]{:S(2)}) collective-permute-start(bf16[320,1024]{1,0:T(8,128)(2,1)} %get-tuple-element.279), channel_id=1, source_target_pairs={{0,8},{8,16},{16,24},{24,32},{32,40},{40,48},{48,56},{56,64},{64,7... | collective-permute-start | bytes 1966088 | tf_op jit(solution)/shard_map/ppermute | solution.py:265
  216.5 11.5 %collective-permute-start.5 = (bf16[320,1024]{1,0:T(8,128)(2,1)}, bf16[320,1024]{1,0:T(8,128)(2,1)S(1)}, u32[]{:S(2)}, u32[]{:S(2)}) collective-permute-start(bf16[320,1024]{1,0:T(8,128)(2,1)} %get-tuple-element.280), channel_id=1, source_target_pairs={{8,0},{16,8},{24,16},{32,24},{40,32},{48,40},{56,48},{64,56},{72,6... | collective-permute-start | bytes 1966088 | tf_op jit(solution)/shard_map/ppermute | solution.py:265
  217.8 12.2 %collective-permute-start.7 = (bf16[320,1024]{1,0:T(8,128)(2,1)}, bf16[320,1024]{1,0:T(8,128)(2,1)}, u32[]{:S(2)}, u32[]{:S(2)}) collective-permute-start(bf16[320,1024]{1,0:T(8,128)(2,1)} %get-tuple-element.281), channel_id=1, source_target_pairs={{1,0},{2,1},{3,2},{4,3},{5,4},{6,5},{7,6},{9,8},{10,9},{11,10},{12... | collective-permute-start | bytes 1966088 | tf_op jit(solution)/shard_map/ppermute | solution.py:265
  219.7 11.5 %collective-permute-start.6 = (bf16[320,1024]{1,0:T(8,128)(2,1)}, bf16[320,1024]{1,0:T(8,128)(2,1)}, u32[]{:S(2)}, u32[]{:S(2)}) collective-permute-start(bf16[320,1024]{1,0:T(8,128)(2,1)} %get-tuple-element.282), channel_id=1, source_target_pairs={{0,1},{1,2},{2,3},{3,4},{4,5},{5,6},{6,7},{8,9},{9,10},{10,11},{11... | collective-permute-start | bytes 1966088 | tf_op jit(solution)/shard_map/ppermute | solution.py:265
  223.4 7.8 %copy-start.7 = (bf16[800,1024]{1,0:T(8,128)(2,1)S(1)}, bf16[800,1024]{1,0:T(8,128)(2,1)}, u32[]{:S(2)}) copy-start(bf16[800,1024]{1,0:T(8,128)(2,1)} %copy-done.6) | copy-start | bytes 4915204
  223.4 7.8 %copy-start.9 = (bf16[800,1024]{1,0:T(8,128)(2,1)S(1)}, bf16[800,1024]{1,0:T(8,128)(2,1)}, u32[]{:S(2)}) copy-start(bf16[800,1024]{1,0:T(8,128)(2,1)} %copy-done.8) | copy-start | bytes 4915204
  226.1 7.1 %copy-start.17 = (bf16[160,1024]{1,0:T(8,128)(2,1)S(1)}, bf16[160,1024]{1,0:T(8,128)(2,1)}, u32[]{:S(2)}) copy-start(bf16[160,1024]{1,0:T(8,128)(2,1)} %param.21) | copy-start | bytes 983044
  233.1 1.6 copy-start.15
  233.1 1.6 copy-start.18

commit v2 on v1

v2 whole, which is shorter than its diff:
```python
import jax
import jax.numpy as jnp
from jax import lax
from jax.experimental import pallas as pl
from jax.experimental.pallas import tpu as pltpu
from jax.sharding import PartitionSpec as P

MESH = pl.DeviceIdType.MESH
F32, BF16 = jnp.float32, jnp.bfloat16
NODE = 160
NEAR = 5 * NODE
PAD = 896
CHUNK = 256
N_CHUNK = 4
DIMS = (0, 1, 2)
ORDERS = ((0, 2, 1), (2, 1, 0), (1, 0, 2))
BIAS_ORDER = (2, 1, 0)


def device_at(coords, core):
    return (coords[0] * 4 + coords[1], coords[2] * 2 + core)


def moved(coords, dim, value):
    return tuple(value if d == dim else c for d, c in enumerate(coords))


def pick(blocks):
    return tuple(blocks.get(d, slice(None)) for d in DIMS)


def partner(half, position):
    return position + 1 - 2 * (position % 2) if half == 0 else 3 - position


def dot(left, right):
    return jnp.dot(left, right, preferred_element_type=F32)


def dot_cols(left, right):
    return lax.dot_general(left, right, (((1,), (1,)), ((), ())), preferred_element_type=F32)


def dot_rows(left, right):
    return lax.dot_general(left, right, (((0,), (0,)), ((), ())), preferred_element_type=F32)


def lanes(start, size):
    return pl.ds(pl.multiple_of(start, 128), size)


def rows(start, size):
    return pl.ds(pl.multiple_of(start, 16), size)


def layer_kernel(
    tokens_hbm, nodes_hbm, dests_ref, count_ref, w_src_hbm, w_dst_hbm, bias_ref, w_out_hbm, cot_hbm,
    updated_ref, token_grad_hbm, node_grad_ref, o_src, o_dst, o_out, o_bias,
    tokens, nodes, w_src, w_dst, w_out, cot, tokens_t, nodes_t, ids, onehot, onehot_t, near, edges,
    back, part, rpart, nsum, nback, grads, stage, bias_sum,
    acc, pair, r1, r2, r3, r4, fin, fin_r, b_acc, b_r,
    in_sem, out_sem, near_s, near_v, part_s, part_v,
    pair_s, pair_v, s1, v1, s2, v2, s3, v3, s4, v4, fin_s, fin_v, b_s, b_v,
):
    region, sub = lax.axis_index("region"), lax.axis_index("sub")
    n_region, n_sub = 16, 8
    coords, core = (region // 4, region % 4, sub // 2), sub % 2
    twin = device_at(coords, 1 - core)
    ring = [
        [device_at(moved(coords, dim, (coords[dim] + hop) % 4), core) for hop in (1, 2, 3)]
        for dim in DIMS
    ]
    around = [
        (region, sub),
        ((region + n_region - 1) % n_region, sub),
        ((region + 1) % n_region, sub),
        (region, (sub + n_sub - 1) % n_sub),
        (region, (sub + 1) % n_sub),
    ]
    facing = (0, 2, 1, 4, 3)
    o_mats = (o_src, o_dst, o_out)
    outs = o_mats
    sends = []

    def remote(source, target, send, recv, device):
        return pltpu.make_async_remote_copy(
            src_ref=source, dst_ref=target, send_sem=send, recv_sem=recv,
            device_id=device, device_id_type=MESH,
        )

    def go(copy):
        copy.start()
        sends.append(copy)
        return copy

    loads = [
        pltpu.make_async_copy(source, target, in_sem.at[i])
        for i, (source, target) in enumerate((
            (nodes_hbm, nodes), (cot_hbm, cot), (w_dst_hbm, w_dst), (w_out_hbm, w_out),
            (w_src_hbm, w_src), (tokens_hbm, tokens),
        ))
    ]
    for load in loads:
        load.start()
    barrier = pltpu.get_barrier_semaphore()
    peers = [twin] + ring[0] + ring[1] + ring[2] + around[1:]
    for peer in peers:
        pl.semaphore_signal(barrier, inc=1, device_id=peer, device_id_type=MESH)

    def near_copy(c, slot):
        return remote(
            near.at[c, pl.ds(0, NODE)], near.at[c, pl.ds(slot * NODE, NODE)],
            near_s.at[c, slot - 1], near_v.at[c, slot - 1], around[facing[slot]],
        )

    def part_copy(c, slot):
        return remote(
            part.at[c, pl.ds(slot * NODE, NODE)], rpart.at[c, facing[slot] - 1],
            part_s.at[c, facing[slot] - 1], part_v.at[c, facing[slot] - 1], around[slot],
        )

    def pair_copy(m, c):
        if m == 2:
            return remote(
                grads.at[2, c, :, :, :, lanes((1 - core) * 512, 512)], pair.at[2, c],
                pair_s.at[2, c], pair_v.at[2, c], twin,
            )
        return remote(
            grads.at[m, :, :, :, :, lanes(c * CHUNK + (1 - core) * 128, 128)],
            pair.at[m, :, :, :, :, lanes(c * 128, 128)],
            pair_s.at[m, c], pair_v.at[m, c], twin,
        )

    for load in loads[:4]:
        load.wait()
    pl.semaphore_wait(barrier, len(peers))

    def project(c, carry):
        span = pl.ds(pl.multiple_of(c * CHUNK, CHUNK), CHUNK)
        near[c, :NODE, :CHUNK] = dot(nodes[...], w_dst[:, span]).astype(BF16)
        near[c, :NODE, CHUNK:] = dot_cols(cot[...], w_out[span, :]).astype(BF16)
        for slot in (1, 2, 3, 4):
            near_copy(c, slot).start()
        near[c, NEAR:, :] = jnp.zeros((PAD - NEAR, 2 * CHUNK), BF16)
        return carry

    lax.fori_loop(0, N_CHUNK, project, 0)

    live = lax.broadcasted_iota(jnp.int32, (2, 1024), 1) < count_ref[0]
    ids[...] = jnp.zeros((8, 1024), jnp.int32)
    ids[:2] = jnp.where(live, dests_ref[...], -1)
    ids_t = ids[...].T
    base = [(around[s][0] * n_sub + around[s][1]) * NODE for s in range(5)]

    def node_ids(shape, dim):
        place = lax.broadcasted_iota(jnp.int32, shape, dim)
        value = jnp.full(shape, -2, jnp.int32)
        for s in range(4, -1, -1):
            value = jnp.where(place < (s + 1) * NODE, place + (base[s] - s * NODE), value)
        return value

    across, down = node_ids((1, PAD), 1), node_ids((NEAR, 1), 0)
    for tb in range(4):
        for k in range(2):
            here = (tb * 2 + k) * 256
            onehot[here : here + 256, :] = jnp.where(
                ids_t[tb * 256 : tb * 256 + 256, k : k + 1] == across, 1.0, 0.0
            ).astype(BF16)
            onehot_t[:, here : here + 256] = jnp.where(
                down == ids[k : k + 1, tb * 256 : tb * 256 + 256], 1.0, 0.0
            ).astype(BF16)
    nodes_t[...] = nodes[...].T
    for load in loads[4:]:
        load.wait()

    def turn(i, carry):
        tokens_t[:, lanes(i * 256, 256)] = tokens[rows(i * 256, 256), :].T
        return carry

    lax.fori_loop(0, 4, turn, 0)
    bias_sum[...] = jnp.zeros((8, 1024), F32)

    def edge_chunk(c):
        span = pl.ds(pl.multiple_of(c * CHUNK, CHUNK), CHUNK)
        for slot in (1, 2, 3, 4):
            near_copy(c, slot).wait_recv()

        def token_block(tb, carry):
            here = rows(tb * 256, 256)
            plain = dot(tokens[here, :], w_src[:, span]) + bias_ref[:, span]
            total = jnp.zeros((256, CHUNK), F32)
            for k in range(2):
                there = rows((tb * 2 + k) * 256, 256)
                found = dot(onehot[there, :], near[c])
                preact = plain + found[:, :CHUNK]
                sigma = 0.5 * jnp.tanh(0.5 * preact) + 0.5
                act = preact * sigma
                grad = found[:, CHUNK:] * (sigma + act * (1.0 - sigma))
                edges[there, :CHUNK] = act.astype(BF16)
                edges[there, CHUNK:] = grad.astype(BF16)
                total = total + grad
            back[here, span] = total.astype(BF16)
            bias_sum[:, span] += jnp.sum(total.reshape(32, 8, CHUNK), axis=0)
            return carry

        lax.fori_loop(0, 4, token_block, 0)

        def scatter(i, carry):
            here = rows(i * 400, 400)
            part[c, here, :] = dot(onehot_t[here, :], edges[...]).astype(BF16)
            return carry

        lax.fori_loop(0, 2, scatter, 0)
        for slot in (1, 2, 3, 4):
            part_copy(c, slot).start()

        def source(z, carry):
            value = dot(tokens_t[rows(z * 256, 256), :], back[:, span])
            grads[0, z, :, :, :, span] = value.astype(BF16).reshape(4, 4, 16, CHUNK)
            return carry

        lax.fori_loop(0, 4, source, 0)
        pair_copy(0, c).start()

    def node_chunk(c):
        span = pl.ds(pl.multiple_of(c * CHUNK, CHUNK), CHUNK)
        total = part[c, :NODE].astype(F32)
        for slot in (1, 2, 3, 4):
            part_copy(c, facing[slot]).wait_recv()
            total = total + rpart[c, slot - 1].astype(F32)
        total = total.astype(BF16)
        nsum[:, span] = total[:, :CHUNK]
        nback[:, span] = total[:, CHUNK:]

        def weight(z, carry):
            value = dot(nodes_t[rows(z * 256, 256), :], nback[:, span])
            grads[1, z, :, :, :, span] = value.astype(BF16).reshape(4, 4, 16, CHUNK)
            return carry

        lax.fori_loop(0, 4, weight, 0)
        pair_copy(1, c).start()
        value = dot_rows(nsum[:, span], cot[...])
        grads[2, c] = value.astype(BF16).reshape(4, 4, 16, 1024)
        pair_copy(2, c).start()

    def chunk(c, carry):
        edge_chunk(c)

        @pl.when(c > 0)
        def _():
            node_chunk(c - 1)

        return carry

    lax.fori_loop(0, N_CHUNK, chunk, 0)

    cols = (pl.ds(0, 256), pl.ds(256, 256))

    def pair_add(m):
        for c in range(N_CHUNK):
            pair_copy(m, c).wait_recv()

        def add_rows(i, carry):
            z, y = i // 4, i % 4
            if m == 2:
                own = grads[m, z, y, :, :, lanes(core * 512, 512)]
                acc[m, z, y] = (own.astype(F32) + pair[m, z, y].astype(F32)).astype(BF16)
            else:
                for c in range(N_CHUNK):
                    own = grads[m, z, y, :, :, lanes(c * CHUNK + core * 128, 128)]
                    part_c = pl.ds(c * 128, 128)
                    other = pair[m, z, y, :, :, part_c]
                    acc[m, z, y, :, :, part_c] = (own.astype(F32) + other.astype(F32)).astype(BF16)
            return carry

        lax.fori_loop(0, 16, add_rows, 0)

    def step_one(m):
        dim = ORDERS[m][0]
        p = coords[dim]
        copies = []
        for half in range(2):
            q = partner(half, p)
            device = device_at(moved(coords, dim, q), core)
            for slot, block in ((1, partner(1 - half, q)), (0, q)):
                copies.append(go(remote(
                    acc.at[(m, *pick({dim: block}), slice(None), cols[half])],
                    r1.at[m, half, slot], s1.at[m, half, slot], v1.at[m, half, slot], device,
                )))
        return copies

    def add_in(m, blocks, half, value_ref):
        where = (m, *pick(blocks), slice(None), cols[half])
        acc[where] = (acc[where].astype(F32) + value_ref[...].astype(F32)).astype(BF16)

    def step_two(m, copies):
        dim = ORDERS[m][0]
        p = coords[dim]
        started = []
        for half in range(2):
            copies[2 * half].wait_recv()
            q = partner(1 - half, p)
            add_in(m, {dim: q}, half, r1.at[m, half, 1])
            started.append(go(remote(
                acc.at[(m, *pick({dim: q}), slice(None), cols[half])],
                r2.at[m, half], s2.at[m, half], v2.at[m, half],
                device_at(moved(coords, dim, q), core),
            )))
        for half in range(2):
            copies[2 * half + 1].wait_recv()
            add_in(m, {dim: p}, half, r1.at[m, half, 0])
        return started

    def step_three(m, copies):
        first, dim = ORDERS[m][0], ORDERS[m][1]
        p = coords[first]
        for half in range(2):
            copies[half].wait_recv()
            add_in(m, {first: p}, half, r2.at[m, half])
        started = []
        for hop in (2, 1, 3):
            block = (coords[dim] + hop) % 4
            started.append(go(remote(
                acc.at[(m, *pick({first: p, dim: block}))],
                r3.at[m, hop - 1], s3.at[m, hop - 1], v3.at[m, hop - 1], ring[dim][hop - 1],
            )))
        return started

    def step_four(m, copies):
        first, second, dim = ORDERS[m]
        for copy in copies:
            copy.wait_recv()
        where = (m, *pick({first: coords[first], second: coords[second]}))
        total = acc[where].astype(F32)
        for slot in range(3):
            total = total + r3[m, slot].astype(F32)
        acc[where] = total.astype(BF16)
        started = []
        for hop in (2, 1, 3):
            block = (coords[dim] + hop) % 4
            started.append(go(remote(
                acc.at[(m, *pick({first: coords[first], second: coords[second], dim: block}))],
                r4.at[m, hop - 1], s4.at[m, hop - 1], v4.at[m, hop - 1], ring[dim][hop - 1],
            )))
        return started

    def step_five(m, copies):
        for copy in copies:
            copy.wait_recv()
        total = acc[(m, *coords)].astype(F32)
        for slot in range(3):
            total = total + r4[m, slot].astype(F32)
        fin[m, 0] = total[:8]
        fin[m, 1] = total[8:]
        return go(remote(fin.at[m, 1 - core], fin_r.at[m], fin_s.at[m], fin_v.at[m], twin))

    def bias_send(stage):
        if stage == 3:
            return [go(remote(b_acc.at[3], b_r.at[9], b_s.at[9], b_v.at[9], twin))]
        started = []
        for hop in range(3):
            slot = 3 * stage + hop
            started.append(go(remote(
                b_acc.at[stage], b_r.at[slot], b_s.at[slot], b_v.at[slot],
                ring[BIAS_ORDER[stage]][hop],
            )))
        return started

    def bias_add(stage, copies):
        total = b_acc[stage]
        for copy in copies:
            copy.wait_recv()
        for slot in range(3 * stage, 3 * stage + len(copies)):
            total = total + b_r[slot]
        return total

    def token_grad_block(i):
        here = pl.ds(i * 256, 256)
        stage[here, :] = dot_cols(back[here, :], w_src[...]).astype(BF16)
        copy = pltpu.make_async_copy(stage.at[here], token_grad_hbm.at[here], out_sem.at[i])
        copy.start()
        return copy

    for i in range(8):
        b_acc[0, i : i + 1, :] = jnp.sum(bias_sum[:, i * 128 : i * 128 + 128], axis=0, keepdims=True)
    b_copies = bias_send(0)
    pair_add(0)
    src = step_one(0)
    written = [token_grad_block(0)]
    node_chunk(N_CHUNK - 1)
    src = step_two(0, src)
    b_acc[1] = bias_add(0, b_copies)
    b_copies = bias_send(1)
    pair_add(1)
    dst = step_one(1)
    pair_add(2)
    out = step_one(2)
    src = step_three(0, src)
    written.append(token_grad_block(1))
    b_acc[2] = bias_add(1, b_copies)
    b_copies = bias_send(2)
    src = step_four(0, src)
    dst = step_two(1, dst)
    out = step_two(2, out)
    written.append(token_grad_block(2))
    src = step_five(0, src)
    b_acc[3] = bias_add(2, b_copies)
    b_copies = bias_send(3)
    dst = step_three(1, dst)
    out = step_three(2, out)
    written.append(token_grad_block(3))
    dst = step_four(1, dst)
    out = step_four(2, out)
    updated_ref[...] = (nodes[...].astype(F32) + dot(nsum[...], w_out[...])).astype(BF16)
    node_grad_ref[...] = (cot[...].astype(F32) + dot_cols(nback[...], w_dst[...])).astype(BF16)
    dst = step_five(1, dst)
    out = step_five(2, out)
    o_bias[...] = bias_add(3, b_copies)
    for m, last in enumerate((src, dst, out)):
        last.wait_recv()
        if m == 2:
            outs[m][:, lanes(core * 512, 512)] = fin[m, core]
            outs[m][:, lanes((1 - core) * 512, 512)] = fin_r[m]
        else:
            for c in range(N_CHUNK):
                part_c = pl.ds(c * 128, 128)
                outs[m][:, lanes(c * CHUNK + core * 128, 128)] = fin[m, core, :, part_c]
                outs[m][:, lanes(c * CHUNK + (1 - core) * 128, 128)] = fin_r[m, :, part_c]
    for copy in written:
        copy.wait()
    for copy in sends:
        copy.wait_send()

    def settle(c, carry):
        for slot in (1, 2, 3, 4):
            near_copy(c, slot).wait_send()
            part_copy(c, slot).wait_send()
        for m in range(3):
            pair_copy(m, c).wait_send()
        return carry

    lax.fori_loop(0, N_CHUNK, settle, 0)


def body(tokens, nodes, dests, token_count, w_src, w_dst, bias, w_out, cotangent):
    dma = pltpu.SemaphoreType.DMA
    vmem = pl.BlockSpec(memory_space=pltpu.VMEM)
    smem = pl.BlockSpec(memory_space=pltpu.SMEM)
    hbm = pl.BlockSpec(memory_space=pl.ANY)
    slab = jax.ShapeDtypeStruct((8, 1024), F32)
    node_like = jax.ShapeDtypeStruct((NODE, 1024), BF16)
    whole = (1024, 1024)
    updated, token_grad, node_grad, o_src, o_dst, o_out, o_bias = pl.pallas_call(
        layer_kernel,
        out_shape=(
            node_like, jax.ShapeDtypeStruct(whole, BF16), node_like, slab, slab, slab,
            jax.ShapeDtypeStruct((8, 128), F32),
        ),
        in_specs=[hbm, hbm, vmem, smem, hbm, hbm, vmem, hbm, hbm],
        out_specs=[vmem, hbm, vmem, vmem, vmem, vmem, vmem],
        scratch_shapes=[
            pltpu.VMEM(whole, BF16), pltpu.VMEM((NODE, 1024), BF16), pltpu.VMEM(whole, BF16),
            pltpu.VMEM(whole, BF16), pltpu.VMEM(whole, BF16), pltpu.VMEM((NODE, 1024), BF16),
            pltpu.VMEM(whole, BF16), pltpu.VMEM((1024, NODE), BF16), pltpu.VMEM((8, 1024), jnp.int32),
            pltpu.VMEM((2048, PAD), BF16), pltpu.VMEM((NEAR, 2048), BF16),
            pltpu.VMEM((N_CHUNK, PAD, 2 * CHUNK), BF16), pltpu.VMEM((2048, 2 * CHUNK), BF16),
            pltpu.VMEM(whole, BF16), pltpu.VMEM((N_CHUNK, NEAR, 2 * CHUNK), BF16),
            pltpu.VMEM((N_CHUNK, 4, NODE, 2 * CHUNK), BF16), pltpu.VMEM((NODE, 1024), BF16),
            pltpu.VMEM((NODE, 1024), BF16), pltpu.VMEM((3, 4, 4, 4, 16, 1024), BF16),
            pltpu.VMEM(whole, BF16), pltpu.VMEM((8, 1024), F32),
            pltpu.VMEM((3, 4, 4, 4, 16, 512), BF16),
            pltpu.VMEM((3, 4, 4, 4, 16, 512), BF16),
            pltpu.VMEM((3, 2, 2, 4, 4, 16, 256), BF16),
            pltpu.VMEM((3, 2, 4, 4, 16, 256), BF16),
            pltpu.VMEM((3, 3, 4, 16, 512), BF16),
            pltpu.VMEM((3, 3, 16, 512), BF16),
            pltpu.VMEM((3, 2, 8, 512), F32),
            pltpu.VMEM((3, 8, 512), F32),
            pltpu.VMEM((4, 8, 128), F32),
            pltpu.VMEM((10, 8, 128), F32),
            dma((6,)), dma((4,)), dma((4, 4)), dma((4, 4)), dma((4, 4)), dma((4, 4)),
            dma((3, 4)), dma((3, 4)), dma((3, 2, 2)), dma((3, 2, 2)), dma((3, 2)), dma((3, 2)),
            dma((3, 3)), dma((3, 3)), dma((3, 3)), dma((3, 3)), dma((3,)), dma((3,)), dma((10,)), dma((10,)),
        ],
        compiler_params=pltpu.CompilerParams(
            collective_id=1, has_side_effects=True, vmem_limit_bytes=60 * 1024 * 1024
        ),
        name="layer",
    )(
        tokens, nodes, dests.T, token_count, w_src, w_dst, bias.reshape(1, 1024), w_out, cotangent,
    )
    index = lax.axis_index("region") * 8 + lax.axis_index("sub")
    part_bias = lax.dynamic_slice(o_bias.reshape(1024), (index * 8,), (8,))
    return updated, token_grad, node_grad, o_src, o_dst, o_out, part_bias


def solution(mesh):
    return jax.shard_map(
        body,
        mesh=mesh,
        in_specs=(
            P(("region", "sub"), None),
            P(("region", "sub"), None),
            P(("region", "sub"), None),
            P(("region", "sub")),
            P(),
            P(),
            P(),
            P(),
            P(("region", "sub"), None),
        ),
        out_specs=(
            P(("region", "sub"), None),
            P(("region", "sub"), None),
            P(("region", "sub"), None),
            P(("region", "sub"), None),
            P(("region", "sub"), None),
            P(("region", "sub"), None),
            P(("region", "sub")),
        ),
        check_vma=False,
    )
```

time: 287 us -> 97 us (0.34)
  local copies, waits for them, and re-layouts: 113 us -> 8.69 us
  Pallas kernels: 45.4 us -> 86.7 us
  matrix products: 36.7 us -> 0 us
  waiting for transfers between devices: 34 us -> 0 us
  other arithmetic: 30.5 us -> 0 us
  starting transfers between devices: 24 us -> 0 us
    gather x8 -> x0, local copies, waits for them, and re-layouts: 47.2 us -> none  [the longest x4 23.6 us: one_block(): upstream = jnp.take(near_up, near_block, axis=0).astype(f32)]
    pallas_call x1, Pallas kernels: 45.4 us -> 86.7 us  [body(): pl.pallas_call(layer_kernel, out_shape=(node_like, jax.ShapeDtypeStruct(w...]
    dot_general x16 -> x0, matrix products: 36.7 us -> none  [the longest x8 22.3 us: contract_rows(): lax.dot_general(left, right, (((0,), (0,)), ((), ())), preferred_element_...]
    ppermute x8 -> x0, waiting for transfers between devices: 34 us -> none  [the longest x2 15.3 us: with_halo(): lax.ppermute(head, axis, [((i + 1) % count, i) for i in range(ends)])]
    ppermute x8 -> x0, starting transfers between devices: 24 us -> none  [the longest x4 11 us: from_behind(): return lax.ppermute(block, axis, route)]
    convert_element_type x4 -> x0, local copies, waits for them, and re-layouts: 17 us -> none  [the longest x2 10.1 us: one_block(): (upstream * sigma * (1.0 + preact * (1.0 - sigma)) * live_mask).astype(bf16)]
    reshape x4 -> x0, local copies, waits for them, and re-layouts: 16.5 us -> none  [the longest x2 8.29 us: one_block(): seg_fwd = seg_fwd + contract_rows(onehot, edge_act.reshape(-1, hidden))]
    reduce_sum x4 -> x0, other arithmetic: 13.4 us -> none  [the longest x2 9.05 us: one_block(): grad_bias = grad_bias + jnp.sum(grad_wide, axis=(0, 1))]
  transfers between devices with their start and end apart: 8 -> 0, of which waited for: 7 -> 0; matrix products, arithmetic and copies ran while one was open for 4% -> 0% of each run, Pallas kernels for 0% -> 0%
where the time goes in v2:
time: 97 us; the launch traced here: 96.7 us
  Pallas kernels  86.7 us (89%)
  local copies, waits for them, and re-layouts  8.69 us (9%)
  between operations  1.31 us (1%)
    pallas_call x1, Pallas kernels, body(): pl.pallas_call(layer_kernel, out_shape=(node_like, jax.ShapeDtypeStruct(w...  86.7 us
    unnamed x14, local copies, waits for them, and re-layouts  7.43 us

profile of v2, /device:TPU:1, one launch (start us, length us, event | category | flops | bytes accessed | tf_op | source)
XLA Modules:
  0.0 96.7 jit_solution(15761240501742221841)
XLA Ops:
  1.3 86.7 %layer.1 = (bf16[160,1024]{1,0:T(8,128)(2,1)}, bf16[1024,1024]{1,0:T(8,128)(2,1)}, bf16[160,1024]{1,0:T(8,128)(2,1)}, f32[8,1024]{1,0:T(8,128)}, f32[8,1024]{1,0...) custom-call(bf16[1024,1024]{1,0:T(8,128)(2,1)} %tokens_hbm.1, bf16[160,1024]{1,0:T(8,128)(2,1)} %nodes_hbm.1, ...), custom_call_target="tpu_custom_call" | custom-call | tf_op jit(solution)/shard_map/layer/pallas_call | solution.py:453
  88.0 1.3 %dynamic_slice.3 = f32[8]{0:T(128)} dynamic-slice(f32[1024]{0:T(1024)} %bitcast.5, s32[]{:T(128)S(6)} %select_n.3), dynamic_slice_sizes={8} | dynamic-slice | bytes 68 | tf_op jit(solution)/shard_map/dynamic_slice | solution.py:493
  89.3 1.7 %copy.23 = bf16[160,1024]{1,0:T(8,128)(2,1)} copy(bf16[160,1024]{1,0:T(8,128)(2,1)} %get-tuple-element.28) | data formatting | bytes 655360
  91.0 0.0 copy-start
  91.0 0.0 copy-start.3
  91.0 0.0 copy-start.2
  91.0 0.0 copy-start.1
  91.0 3.1 %copy.24 = bf16[1024,1024]{1,0:T(8,128)(2,1)} copy(bf16[1024,1024]{1,0:T(8,128)(2,1)} %get-tuple-element.29) | data formatting | bytes 4194304
  94.2 0.0 copy-done
  94.2 0.7 copy.25
  94.9 0.0 copy-done.3
  94.9 0.6 copy.26
  95.5 0.0 copy-done.2
  95.5 0.6 copy.27
  96.1 0.0 copy-done.1
  96.1 0.6 copy.28
Async XLA Ops:
  91.0 3.1 %copy-start = (bf16[160,1024]{1,0:T(8,128)(2,1)S(1)}, bf16[160,1024]{1,0:T(8,128)(2,1)}, u32[]{:S(2)}) copy-start(bf16[160,1024]{1,0:T(8,128)(2,1)} %get-tuple-element.30) | copy-start | bytes 983044
  91.0 3.9 %copy-start.3 = (f32[8,1024]{1,0:T(8,128)S(1)}, f32[8,1024]{1,0:T(8,128)}, u32[]{:S(2)}) copy-start(f32[8,1024]{1,0:T(8,128)} %get-tuple-element.31) | copy-start | bytes 98308
  91.0 4.5 %copy-start.2 = (f32[8,1024]{1,0:T(8,128)S(1)}, f32[8,1024]{1,0:T(8,128)}, u32[]{:S(2)}) copy-start(f32[8,1024]{1,0:T(8,128)} %get-tuple-element.32) | copy-start | bytes 98308
  91.0 5.1 %copy-start.1 = (f32[8,1024]{1,0:T(8,128)S(1)}, f32[8,1024]{1,0:T(8,128)}, u32[]{:S(2)}) copy-start(f32[8,1024]{1,0:T(8,128)} %get-tuple-element.33) | copy-start | bytes 98308

commit v3 on v2

--- a/solution.py
+++ b/solution.py
@@ -13,8 +13,9 @@
 CHUNK = 256
 N_CHUNK = 4
 DIMS = (0, 1, 2)
-ORDERS = ((0, 2, 1), (2, 1, 0), (1, 0, 2))
+ORDERS = ((2, 0, 1), (0, 1, 2), (1, 2, 0))
 BIAS_ORDER = (2, 1, 0)
+HOPS = (2, 1, 3)
 
 
 def device_at(coords, core):
@@ -27,10 +28,6 @@
 
 def pick(blocks):
     return tuple(blocks.get(d, slice(None)) for d in DIMS)
-
-
-def partner(half, position):
-    return position + 1 - 2 * (position % 2) if half == 0 else 3 - position
 
 
 def dot(left, right):
@@ -58,9 +55,9 @@
     updated_ref, token_grad_hbm, node_grad_ref, o_src, o_dst, o_out, o_bias,
     tokens, nodes, w_src, w_dst, w_out, cot, tokens_t, nodes_t, ids, onehot, onehot_t, near, edges,
     back, part, rpart, nsum, nback, grads, stage, bias_sum,
-    acc, pair, r1, r2, r3, r4, fin, fin_r, b_acc, b_r,
+    acc, pair, r1, r2, r3, fin, fin_r, b_acc, b_r,
     in_sem, out_sem, near_s, near_v, part_s, part_v,
-    pair_s, pair_v, s1, v1, s2, v2, s3, v3, s4, v4, fin_s, fin_v, b_s, b_v,
+    pair_s, pair_v, s1, v1, s2, v2, s3, v3, fin_s, fin_v, b_s, b_v,
 ):
     region, sub = lax.axis_index("region"), lax.axis_index("sub")
     n_region, n_sub = 16, 8
@@ -78,8 +75,7 @@
         (region, (sub + 1) % n_sub),
     ]
     facing = (0, 2, 1, 4, 3)
-    o_mats = (o_src, o_dst, o_out)
-    outs = o_mats
+    outs = (o_src, o_dst, o_out)
     sends = []
 
     def remote(source, target, send, recv, device):
@@ -131,22 +127,7 @@
             pair_s.at[m, c], pair_v.at[m, c], twin,
         )
 
-    for load in loads[:4]:
-        load.wait()
-    pl.semaphore_wait(barrier, len(peers))
-
-    def project(c, carry):
-        span = pl.ds(pl.multiple_of(c * CHUNK, CHUNK), CHUNK)
-        near[c, :NODE, :CHUNK] = dot(nodes[...], w_dst[:, span]).astype(BF16)
-        near[c, :NODE, CHUNK:] = dot_cols(cot[...], w_out[span, :]).astype(BF16)
-        for slot in (1, 2, 3, 4):
-            near_copy(c, slot).start()
-        near[c, NEAR:, :] = jnp.zeros((PAD - NEAR, 2 * CHUNK), BF16)
-        return carry
-
-    lax.fori_loop(0, N_CHUNK, project, 0)
-
-    live = lax.broadcasted_iota(jnp.int32, (2, 1024), 1) < count_ref[0]
+    live = lax.broadcasted_iota(jnp.int32, (2, 1024), 1) < count_ref[...]
     ids[...] = jnp.zeros((8, 1024), jnp.int32)
     ids[:2] = jnp.where(live, dests_ref[...], -1)
     ids_t = ids[...].T
@@ -169,6 +150,22 @@
             onehot_t[:, here : here + 256] = jnp.where(
                 down == ids[k : k + 1, tb * 256 : tb * 256 + 256], 1.0, 0.0
             ).astype(BF16)
+
+    for load in loads[:4]:
+        load.wait()
+    pl.semaphore_wait(barrier, len(peers))
+
+    def project(c, carry):
+        span = pl.ds(pl.multiple_of(c * CHUNK, CHUNK), CHUNK)
+        near[c, :NODE, :CHUNK] = dot(nodes[...], w_dst[:, span]).astype(BF16)
+        near[c, :NODE, CHUNK:] = dot_cols(cot[...], w_out[span, :]).astype(BF16)
+        for slot in (1, 2, 3, 4):
+            near_copy(c, slot).start()
+        near[c, NEAR:, :] = jnp.zeros((PAD - NEAR, 2 * CHUNK), BF16)
+        return carry
+
+    lax.fori_loop(0, N_CHUNK, project, 0)
+
     nodes_t[...] = nodes[...].T
     for load in loads[4:]:
         load.wait()
@@ -203,23 +200,14 @@
             bias_sum[:, span] += jnp.sum(total.reshape(32, 8, CHUNK), axis=0)
             return carry
 
-        lax.fori_loop(0, 4, token_block, 0)
-
-        def scatter(i, carry):
-            here = rows(i * 400, 400)
-            part[c, here, :] = dot(onehot_t[here, :], edges[...]).astype(BF16)
-            return carry
-
-        lax.fori_loop(0, 2, scatter, 0)
+        lax.fori_loop(0, 4, token_block, 0, unroll=2)
+
+        part[c] = dot(onehot_t[...], edges[...]).astype(BF16)
         for slot in (1, 2, 3, 4):
             part_copy(c, slot).start()
 
-        def source(z, carry):
-            value = dot(tokens_t[rows(z * 256, 256), :], back[:, span])
-            grads[0, z, :, :, :, span] = value.astype(BF16).reshape(4, 4, 16, CHUNK)
-            return carry
-
-        lax.fori_loop(0, 4, source, 0)
+        value = dot(tokens_t[...], back[:, span])
+        grads[0, :, :, :, :, span] = value.astype(BF16).reshape(4, 4, 4, 16, CHUNK)
         pair_copy(0, c).start()
 
     def node_chunk(c):
@@ -232,127 +220,132 @@
         nsum[:, span] = total[:, :CHUNK]
         nback[:, span] = total[:, CHUNK:]
 
-        def weight(z, carry):
-            value = dot(nodes_t[rows(z * 256, 256), :], nback[:, span])
-            grads[1, z, :, :, :, span] = value.astype(BF16).reshape(4, 4, 16, CHUNK)
-            return carry
-
-        lax.fori_loop(0, 4, weight, 0)
+        value = dot(nodes_t[...], nback[:, span])
+        grads[1, :, :, :, :, span] = value.astype(BF16).reshape(4, 4, 4, 16, CHUNK)
         pair_copy(1, c).start()
         value = dot_rows(nsum[:, span], cot[...])
         grads[2, c] = value.astype(BF16).reshape(4, 4, 16, 1024)
         pair_copy(2, c).start()
 
+    def pair_add(m, c):
+        pair_copy(m, c).wait_recv()
+        if m == 2:
+            own = grads[2, c, :, :, :, lanes(core * 512, 512)].astype(F32)
+            acc[2, c] = (own + pair[2, c].astype(F32)).astype(BF16)
+            return
+        here = lanes(c * 128, 128)
+        own = grads[m, :, :, :, :, lanes(c * CHUNK + core * 128, 128)].astype(F32)
+        acc[m, :, :, :, :, here] = (own + pair[m, :, :, :, :, here].astype(F32)).astype(BF16)
+
+    def first_copy(m, c, hop):
+        dim = ORDERS[m][0]
+        block = (coords[dim] + hop) % 4
+        if m == 2:
+            source, target = acc.at[2, c, block], r1.at[2, hop - 1, c]
+        else:
+            here = lanes(c * 128, 128)
+            source = acc.at[(m, *pick({dim: block}), slice(None), here)]
+            target = r1.at[m, hop - 1, :, :, :, here]
+        return remote(source, target, s1.at[m, c, hop - 1], v1.at[m, c, hop - 1], ring[dim][hop - 1])
+
+    def second_copy(m, c, hop):
+        done, dim = ORDERS[m][:2]
+        block = (coords[dim] + hop) % 4
+        if m == 2:
+            source, target = acc.at[2, c, coords[done], block], r2.at[2, hop - 1, c]
+        else:
+            here = lanes(c * 128, 128)
+            source = acc.at[(m, *pick({done: coords[done], dim: block}), slice(None), here)]
+            target = r2.at[m, hop - 1, :, :, here]
+        return remote(source, target, s2.at[m, c, hop - 1], v2.at[m, c, hop - 1], ring[dim][hop - 1])
+
+    def third_copy(m, hop):
+        one, two, dim = ORDERS[m]
+        block = (coords[dim] + hop) % 4
+        source = acc.at[(m, *pick({one: coords[one], two: coords[two], dim: block}))]
+        return remote(source, r3.at[m, hop - 1], s3.at[m, hop - 1], v3.at[m, hop - 1], ring[dim][hop - 1])
+
+    def first_send(m, c):
+        pair_add(m, c)
+        for hop in HOPS:
+            first_copy(m, c, hop).start()
+
+    def second_send(m, c):
+        dim = ORDERS[m][0]
+        for hop in HOPS:
+            first_copy(m, c, hop).wait_recv()
+        if m == 2:
+            total = acc[2, c, coords[dim]].astype(F32)
+            for slot in range(3):
+                total = total + r1[2, slot, c].astype(F32)
+            acc[2, c, coords[dim]] = total.astype(BF16)
+        else:
+            here = lanes(c * 128, 128)
+            where = (m, *pick({dim: coords[dim]}), slice(None), here)
+            total = acc[where].astype(F32)
+            for slot in range(3):
+                total = total + r1[m, slot, :, :, :, here].astype(F32)
+            acc[where] = total.astype(BF16)
+        for hop in HOPS:
+            second_copy(m, c, hop).start()
+
+    def second_add(m, c):
+        one, two = ORDERS[m][:2]
+        for hop in HOPS:
+            second_copy(m, c, hop).wait_recv()
+        if m == 2:
+            where = (2, c, coords[one], coords[two])
+            total = acc[where].astype(F32)
+            for slot in range(3):
+                total = total + r2[2, slot, c].astype(F32)
+        else:
+            here = lanes(c * 128, 128)
+            where = (m, *pick({one: coords[one], two: coords[two]}), slice(None), here)
+            total = acc[where].astype(F32)
+            for slot in range(3):
+                total = total + r2[m, slot, :, :, here].astype(F32)
+        acc[where] = total.astype(BF16)
+
+    def third_send(m):
+        for hop in HOPS:
+            third_copy(m, hop).start()
+
+    def last_send(m):
+        for hop in HOPS:
+            third_copy(m, hop).wait_recv()
+        total = acc[(m, *coords)].astype(F32)
+        for slot in range(3):
+            total = total + r3[m, slot].astype(F32)
+        fin[m, 0] = total[:8]
+        fin[m, 1] = total[8:]
+        last_copy(m).start()
+
+    def last_copy(m):
+        return remote(fin.at[m, 1 - core], fin_r.at[m], fin_s.at[m], fin_v.at[m], twin)
+
     def chunk(c, carry):
         edge_chunk(c)
 
         @pl.when(c > 0)
         def _():
             node_chunk(c - 1)
+            first_send(0, c - 1)
+
+        @pl.when(c > 1)
+        def _():
+            first_send(1, c - 2)
+            first_send(2, c - 2)
+            second_send(0, c - 2)
+
+        @pl.when(c > 2)
+        def _():
+            second_send(1, c - 3)
+            second_send(2, c - 3)
+            second_add(0, c - 3)
 
         return carry
 
     lax.fori_loop(0, N_CHUNK, chunk, 0)
-
-    cols = (pl.ds(0, 256), pl.ds(256, 256))
-
-    def pair_add(m):
-        for c in range(N_CHUNK):
-            pair_copy(m, c).wait_recv()
-
-        def add_rows(i, carry):
-            z, y = i // 4, i % 4
-            if m == 2:
-                own = grads[m, z, y, :, :, lanes(core * 512, 512)]
-                acc[m, z, y] = (own.astype(F32) + pair[m, z, y].astype(F32)).astype(BF16)
-            else:
-                for c in range(N_CHUNK):
-                    own = grads[m, z, y, :, :, lanes(c * CHUNK + core * 128, 128)]
-                    part_c = pl.ds(c * 128, 128)
-                    other = pair[m, z, y, :, :, part_c]
-                    acc[m, z, y, :, :, part_c] = (own.astype(F32) + other.astype(F32)).astype(BF16)
-            return carry
-
-        lax.fori_loop(0, 16, add_rows, 0)
-
-    def step_one(m):
-        dim = ORDERS[m][0]
-        p = coords[dim]
-        copies = []
-        for half in range(2):
-            q = partner(half, p)
-            device = device_at(moved(coords, dim, q), core)
-            for slot, block in ((1, partner(1 - half, q)), (0, q)):
-                copies.append(go(remote(
-                    acc.at[(m, *pick({dim: block}), slice(None), cols[half])],
-                    r1.at[m, half, slot], s1.at[m, half, slot], v1.at[m, half, slot], device,
-                )))
-        return copies
-
-    def add_in(m, blocks, half, value_ref):
-        where = (m, *pick(blocks), slice(None), cols[half])
-        acc[where] = (acc[where].astype(F32) + value_ref[...].astype(F32)).astype(BF16)
-
-    def step_two(m, copies):
-        dim = ORDERS[m][0]
-        p = coords[dim]
-        started = []
-        for half in range(2):
-            copies[2 * half].wait_recv()
-            q = partner(1 - half, p)
-            add_in(m, {dim: q}, half, r1.at[m, half, 1])
-            started.append(go(remote(
-                acc.at[(m, *pick({dim: q}), slice(None), cols[half])],
-                r2.at[m, half], s2.at[m, half], v2.at[m, half],
-                device_at(moved(coords, dim, q), core),
-            )))
-        for half in range(2):
-            copies[2 * half + 1].wait_recv()
-            add_in(m, {dim: p}, half, r1.at[m, half, 0])
-        return started
-
-    def step_three(m, copies):
-        first, dim = ORDERS[m][0], ORDERS[m][1]
-        p = coords[first]
-        for half in range(2):
-            copies[half].wait_recv()
-            add_in(m, {first: p}, half, r2.at[m, half])
-        started = []
-        for hop in (2, 1, 3):
-            block = (coords[dim] + hop) % 4
-            started.append(go(remote(
-                acc.at[(m, *pick({first: p, dim: block}))],
-                r3.at[m, hop - 1], s3.at[m, hop - 1], v3.at[m, hop - 1], ring[dim][hop - 1],
-            )))
-        return started
-
-    def step_four(m, copies):
-        first, second, dim = ORDERS[m]
-        for copy in copies:
-            copy.wait_recv()
-        where = (m, *pick({first: coords[first], second: coords[second]}))
-        total = acc[where].astype(F32)
-        for slot in range(3):
-            total = total + r3[m, slot].astype(F32)
-        acc[where] = total.astype(BF16)
-        started = []
-        for hop in (2, 1, 3):
-            block = (coords[dim] + hop) % 4
-            started.append(go(remote(
-                acc.at[(m, *pick({first: coords[first], second: coords[second], dim: block}))],
-                r4.at[m, hop - 1], s4.at[m, hop - 1], v4.at[m, hop - 1], ring[dim][hop - 1],
-            )))
-        return started
-
-    def step_five(m, copies):
-        for copy in copies:
-            copy.wait_recv()
-        total = acc[(m, *coords)].astype(F32)
-        for slot in range(3):
-            total = total + r4[m, slot].astype(F32)
-        fin[m, 0] = total[:8]
-        fin[m, 1] = total[8:]
-        return go(remote(fin.at[m, 1 - core], fin_r.at[m], fin_s.at[m], fin_v.at[m], twin))
 
     def bias_send(stage):
         if stage == 3:
@@ -384,40 +377,51 @@
     for i in range(8):
         b_acc[0, i : i + 1, :] = jnp.sum(bias_sum[:, i * 128 : i * 128 + 128], axis=0, keepdims=True)
     b_copies = bias_send(0)
-    pair_add(0)
-    src = step_one(0)
+    first_send(0, 3)
+    first_send(1, 2)
+    first_send(2, 2)
+    second_send(0, 2)
+    second_send(1, 1)
+    second_send(2, 1)
     written = [token_grad_block(0)]
-    node_chunk(N_CHUNK - 1)
-    src = step_two(0, src)
+    node_chunk(3)
     b_acc[1] = bias_add(0, b_copies)
     b_copies = bias_send(1)
-    pair_add(1)
-    dst = step_one(1)
-    pair_add(2)
-    out = step_one(2)
-    src = step_three(0, src)
     written.append(token_grad_block(1))
+    first_send(1, 3)
+    first_send(2, 3)
+    second_send(0, 3)
+    second_send(1, 2)
+    second_send(2, 2)
     b_acc[2] = bias_add(1, b_copies)
     b_copies = bias_send(2)
-    src = step_four(0, src)
-    dst = step_two(1, dst)
-    out = step_two(2, out)
+    second_add(0, 1)
+    second_add(0, 2)
+    second_add(1, 0)
+    second_add(2, 0)
     written.append(token_grad_block(2))
-    src = step_five(0, src)
+    second_send(1, 3)
+    second_send(2, 3)
+    second_add(0, 3)
+    third_send(0)
     b_acc[3] = bias_add(2, b_copies)
     b_copies = bias_send(3)
-    dst = step_three(1, dst)
-    out = step_three(2, out)
+    second_add(1, 1)
+    second_add(2, 1)
+    second_add(1, 2)
+    second_add(2, 2)
     written.append(token_grad_block(3))
-    dst = step_four(1, dst)
-    out = step_four(2, out)
+    second_add(1, 3)
+    third_send(1)
+    second_add(2, 3)
+    third_send(2)
     updated_ref[...] = (nodes[...].astype(F32) + dot(nsum[...], w_out[...])).astype(BF16)
     node_grad_ref[...] = (cot[...].astype(F32) + dot_cols(nback[...], w_dst[...])).astype(BF16)
-    dst = step_five(1, dst)
-    out = step_five(2, out)
     o_bias[...] = bias_add(3, b_copies)
-    for m, last in enumerate((src, dst, out)):
-        last.wait_recv()
+    for m in range(3):
+        last_send(m)
+    for m in range(3):
+        last_copy(m).wait_recv()
         if m == 2:
             outs[m][:, lanes(core * 512, 512)] = fin[m, core]
             outs[m][:, lanes((1 - core) * 512, 512)] = fin_r[m]
@@ -437,15 +441,58 @@
             part_copy(c, slot).wait_send()
         for m in range(3):
             pair_copy(m, c).wait_send()
+            for hop in HOPS:
+                first_copy(m, c, hop).wait_send()
+                second_copy(m, c, hop).wait_send()
         return carry
 
     lax.fori_loop(0, N_CHUNK, settle, 0)
+    for m in range(3):
+        last_copy(m).wait_send()
+        for hop in HOPS:
+            third_copy(m, hop).wait_send()
+
+
+def finish_kernel(*refs):
+    ins, b_ref, outs, o_ref, sems = refs[:6], refs[6], refs[7:13], refs[13], refs[14]
+    copies = []
+    for i, (source, target) in enumerate(zip(ins, outs)):
+        pieces = 4 if source.shape[0] == 1024 else 1
+        size = source.shape[0] // pieces
+        for piece in range(pieces):
+            here = pl.ds(piece * size, size)
+            copies.append(pltpu.make_async_copy(source.at[here], target.at[here], sems.at[i, piece]))
+    for copy in copies:
+        copy.start()
+    index = lax.axis_index("region") * 8 + lax.axis_index("sub")
+    turned = pltpu.roll(b_ref[...], (128 - index % 16 * 8) % 128, axis=1)
+    own = lax.broadcasted_iota(jnp.int32, (8, 128), 0) == index // 16
+    o_ref[...] = jnp.sum(jnp.where(own, turned, 0.0), axis=0, keepdims=True)[:, :8]
+    for copy in copies:
+        copy.wait()
+
+
+def finish(arrays, bias_sums):
+    vmem = pl.BlockSpec(memory_space=pltpu.VMEM)
+    hbm = pl.BlockSpec(memory_space=pl.ANY)
+    *results, part_bias = pl.pallas_call(
+        finish_kernel,
+        out_shape=(
+            *[jax.ShapeDtypeStruct(a.shape, a.dtype) for a in arrays],
+            jax.ShapeDtypeStruct((1, 8), F32),
+        ),
+        in_specs=[hbm] * 6 + [vmem],
+        out_specs=[hbm] * 6 + [vmem],
+        scratch_shapes=[pltpu.SemaphoreType.DMA((6, 4))],
+        compiler_params=pltpu.CompilerParams(vmem_limit_bytes=60 * 1024 * 1024),
+        name="finish",
+    )(*arrays, bias_sums)
+    return (*results, part_bias.reshape(8))
 
 
 def body(tokens, nodes, dests, token_count, w_src, w_dst, bias, w_out, cotangent):
     dma = pltpu.SemaphoreType.DMA
     vmem = pl.BlockSpec(memory_space=pltpu.VMEM)
-    smem = pl.BlockSpec(memory_space=pltpu.SMEM)
     hbm = pl.BlockSpec(memory_space=pl.ANY)
     slab = jax.ShapeDtypeStruct((8, 1024), F32)
     node_like = jax.ShapeDtypeStruct((NODE, 1024), BF16)
@@ -456,7 +503,7 @@
             node_like, jax.ShapeDtypeStruct(whole, BF16), node_like, slab, slab, slab,
             jax.ShapeDtypeStruct((8, 128), F32),
         ),
-        in_specs=[hbm, hbm, vmem, smem, hbm, hbm, vmem, hbm, hbm],
+        in_specs=[hbm, hbm, vmem, vmem, hbm, hbm, vmem, hbm, hbm],
         out_specs=[vmem, hbm, vmem, vmem, vmem, vmem, vmem],
         scratch_shapes=[
             pltpu.VMEM(whole, BF16), pltpu.VMEM((NODE, 1024), BF16), pltpu.VMEM(whole, BF16),
@@ -470,8 +517,7 @@
             pltpu.VMEM(whole, BF16), pltpu.VMEM((8, 1024), F32),
             pltpu.VMEM((3, 4, 4, 4, 16, 512), BF16),
             pltpu.VMEM((3, 4, 4, 4, 16, 512), BF16),
-            pltpu.VMEM((3, 2, 2, 4, 4, 16, 256), BF16),
-            pltpu.VMEM((3, 2, 4, 4, 16, 256), BF16),
+            pltpu.VMEM((3, 3, 4, 4, 16, 512), BF16),
             pltpu.VMEM((3, 3, 4, 16, 512), BF16),
             pltpu.VMEM((3, 3, 16, 512), BF16),
             pltpu.VMEM((3, 2, 8, 512), F32),
@@ -479,19 +525,17 @@
             pltpu.VMEM((4, 8, 128), F32),
             pltpu.VMEM((10, 8, 128), F32),
             dma((6,)), dma((4,)), dma((4, 4)), dma((4, 4)), dma((4, 4)), dma((4, 4)),
-            dma((3, 4)), dma((3, 4)), dma((3, 2, 2)), dma((3, 2, 2)), dma((3, 2)), dma((3, 2)),
-            dma((3, 3)), dma((3, 3)), dma((3, 3)), dma((3, 3)), dma((3,)), dma((3,)), dma((10,)), dma((10,)),
+            dma((3, 4)), dma((3, 4)), dma((3, 4, 3)), dma((3, 4, 3)), dma((3, 4, 3)), dma((3, 4, 3)),
+            dma((3, 3)), dma((3, 3)), dma((3,)), dma((3,)), dma((10,)), dma((10,)),
         ],
         compiler_params=pltpu.CompilerParams(
             collective_id=1, has_side_effects=True, vmem_limit_bytes=60 * 1024 * 1024
         ),
         name="layer",
     )(
-        tokens, nodes, dests.T, token_count, w_src, w_dst, bias.reshape(1, 1024), w_out, cotangent,
+        tokens, nodes, dests.T, token_count.reshape(1, 1), w_src, w_dst, bias.reshape(1, 1024), w_out, cotangent,
     )
-    index = lax.axis_index("region") * 8 + lax.axis_index("sub")
-    part_bias = lax.dynamic_slice(o_bias.reshape(1024), (index * 8,), (8,))
-    return updated, token_grad, node_grad, o_src, o_dst, o_out, part_bias
+    return finish((updated, token_grad, node_grad, o_src, o_dst, o_out), o_bias)
 
 
 def solution(mesh):

time: 97 us -> 166 us (1.71)
  Pallas kernels: 86.7 us -> 164 us
  local copies, waits for them, and re-layouts: 8.69 us -> 0 us
    pallas_call x0 -> x1, Pallas kernels: none -> 88.9 us  [finish(): pl.pallas_call(finish_kernel, out_shape=(*[jax.ShapeDtypeStruct(a.shape,...]
    pallas_call x1, Pallas kernels: 86.7 us -> 75 us  [body(): pl.pallas_call(layer_kernel, out_shape=(node_like, jax.ShapeDtypeStruct(w...]
    unnamed x14 -> x0, local copies, waits for them, and re-layouts: 7.43 us -> none
where the time goes in v3:
time: 166 us; the launch traced here: 165 us
  Pallas kernels  164 us (99%)
    pallas_call x1, Pallas kernels, finish(): pl.pallas_call(finish_kernel, out_shape=(*[jax.ShapeDtypeStruct(a.shape,...  88.9 us
    pallas_call x1, Pallas kernels, body(): pl.pallas_call(layer_kernel, out_shape=(node_like, jax.ShapeDtypeStruct(w...  75 us

profile of v3, /device:TPU:1, one launch (start us, length us, event | category | flops | bytes accessed | tf_op | source)
XLA Modules:
  0.0 165.3 jit_solution(14173780053720405785)
XLA Ops:
  1.3 75.0 %layer.1 = (bf16[160,1024]{1,0:T(8,128)(2,1)}, bf16[1024,1024]{1,0:T(8,128)(2,1)}, bf16[160,1024]{1,0:T(8,128)(2,1)}, f32[8,1024]{1,0:T(8,128)}, f32[8,1024]{1,0...) custom-call(bf16[1024,1024]{1,0:T(8,128)(2,1)} %tokens_hbm.1, bf16[160,1024]{1,0:T(8,128)(2,1)} %nodes_hbm.1, ...), custom_call_target="tpu_custom_call" | custom-call | tf_op jit(solution)/shard_map/layer/pallas_call | solution.py:500
  76.3 88.9 %finish.1 = (bf16[160,1024]{1,0:T(8,128)(2,1)}, bf16[1024,1024]{1,0:T(8,128)(2,1)}, bf16[160,1024]{1,0:T(8,128)(2,1)}, f32[8,1024]{1,0:T(8,128)}, f32[8,1024]{1,...) custom-call(bf16[160,1024]{1,0:T(8,128)(2,1)} %get-tuple-element.21.refs_0_, ...), custom_call_target="tpu_custom_call" | custom-call | tf_op jit(solution)/shard_map/finish/pallas_call | solution.py:478

commit v4 on v3

--- a/solution.py
+++ b/solution.py
@@ -454,22 +454,28 @@
 
 
 def finish_kernel(*refs):
-    ins, b_ref, outs, o_ref, sems = refs[:6], refs[6], refs[7:13], refs[13], refs[14]
+    ins, b_ref, outs, o_ref, held, in_sems, out_sems = refs[:6], refs[6], refs[7:13], refs[13], refs[14:20], refs[20], refs[21]
     copies = []
     for i, (source, target) in enumerate(zip(ins, outs)):
         pieces = 4 if source.shape[0] == 1024 else 1
         size = source.shape[0] // pieces
         for piece in range(pieces):
             here = pl.ds(piece * size, size)
-            copies.append(pltpu.make_async_copy(source.at[here], target.at[here], sems.at[i, piece]))
-    for copy in copies:
-        copy.start()
+            copies.append((
+                pltpu.make_async_copy(source.at[here], held[i].at[here], in_sems.at[i, piece]),
+                pltpu.make_async_copy(held[i].at[here], target.at[here], out_sems.at[i, piece]),
+            ))
+    for fetch, _ in copies:
+        fetch.start()
     index = lax.axis_index("region") * 8 + lax.axis_index("sub")
     turned = pltpu.roll(b_ref[...], (128 - index % 16 * 8) % 128, axis=1)
     own = lax.broadcasted_iota(jnp.int32, (8, 128), 0) == index // 16
     o_ref[...] = jnp.sum(jnp.where(own, turned, 0.0), axis=0, keepdims=True)[:, :8]
-    for copy in copies:
-        copy.wait()
+    for fetch, store in copies:
+        fetch.wait()
+        store.start()
+    for _, store in copies:
+        store.wait()
 
 
 def finish(arrays, bias_sums):
@@ -483,7 +489,10 @@
         ),
         in_specs=[hbm] * 6 + [vmem],
         out_specs=[hbm] * 6 + [vmem],
-        scratch_shapes=[pltpu.SemaphoreType.DMA((6, 4))],
+        scratch_shapes=[
+            *[pltpu.VMEM(a.shape, a.dtype) for a in arrays],
+            pltpu.SemaphoreType.DMA((6, 4)), pltpu.SemaphoreType.DMA((6, 4)),
+        ],
         compiler_params=pltpu.CompilerParams(vmem_limit_bytes=60 * 1024 * 1024),
         name="finish",
     )(*arrays, bias_sums)

time: 166 us -> 80.9 us (0.49)
  Pallas kernels: 164 us -> 79.2 us
    pallas_call x1, Pallas kernels: 88.9 us -> 4.19 us  [finish(): pl.pallas_call(finish_kernel, out_shape=(*[jax.ShapeDtypeStruct(a.shape,...]
where the time goes in v4:
time: 80.9 us; the launch traced here: 80.7 us
  Pallas kernels  79.2 us (98%)
  between operations  1.45 us (2%)
    pallas_call x1, Pallas kernels, body(): pl.pallas_call(layer_kernel, out_shape=(node_like, jax.ShapeDtypeStruct(w...  75 us
    pallas_call x1, Pallas kernels, finish(): pl.pallas_call(finish_kernel, out_shape=(*[jax.ShapeDtypeStruct(a.shape,...  4.19 us

profile of v4, /device:TPU:1, one launch (start us, length us, event | category | flops | bytes accessed | tf_op | source)
XLA Modules:
  0.0 80.7 jit_solution(4037249635611016930)
XLA Ops:
  1.3 75.0 %layer.1 = (bf16[160,1024]{1,0:T(8,128)(2,1)}, bf16[1024,1024]{1,0:T(8,128)(2,1)}, bf16[160,1024]{1,0:T(8,128)(2,1)}, f32[8,1024]{1,0:T(8,128)}, f32[8,1024]{1,0...) custom-call(bf16[1024,1024]{1,0:T(8,128)(2,1)} %tokens_hbm.1, bf16[160,1024]{1,0:T(8,128)(2,1)} %nodes_hbm.1, ...), custom_call_target="tpu_custom_call" | custom-call | tf_op jit(solution)/shard_map/layer/pallas_call | solution.py:509
  76.3 4.2 %finish.1 = (bf16[160,1024]{1,0:T(8,128)(2,1)}, bf16[1024,1024]{1,0:T(8,128)(2,1)}, bf16[160,1024]{1,0:T(8,128)(2,1)}, f32[8,1024]{1,0:T(8,128)}, f32[8,1024]{1,...) custom-call(bf16[160,1024]{1,0:T(8,128)(2,1)} %get-tuple-element.21.refs_0_, ...), custom_call_target="tpu_custom_call" | custom-call | tf_op jit(solution)/shard_map/finish/pallas_call | solution.py:484

commit v5 on v4

--- a/solution.py
+++ b/solution.py
@@ -96,7 +96,7 @@
             (w_src_hbm, w_src), (tokens_hbm, tokens),
         ))
     ]
-    for load in loads:
+    for load in loads[:4]:
         load.start()
     barrier = pltpu.get_barrier_semaphore()
     peers = [twin] + ring[0] + ring[1] + ring[2] + around[1:]
@@ -127,6 +127,28 @@
             pair_s.at[m, c], pair_v.at[m, c], twin,
         )
 
+    def project(c):
+        span = pl.ds(pl.multiple_of(c * CHUNK, CHUNK), CHUNK)
+        near[c, :NODE, :CHUNK] = dot(nodes[...], w_dst[:, span]).astype(BF16)
+        near[c, :NODE, CHUNK:] = dot_cols(cot[...], w_out[span, :]).astype(BF16)
+        near[c, NEAR:, :] = jnp.zeros((PAD - NEAR, 2 * CHUNK), BF16)
+
+    def send_near(c):
+        for slot in (1, 2, 3, 4):
+            near_copy(c, slot).start()
+
+    def project_later(c, carry):
+        project(c)
+        return carry
+
+    for load in loads[:4]:
+        load.wait()
+    for load in loads[4:]:
+        load.start()
+    project(0)
+    pl.semaphore_wait(barrier, len(peers))
+    send_near(0)
+
     live = lax.broadcasted_iota(jnp.int32, (2, 1024), 1) < count_ref[...]
     ids[...] = jnp.zeros((8, 1024), jnp.int32)
     ids[:2] = jnp.where(live, dests_ref[...], -1)
@@ -143,7 +165,7 @@
     across, down = node_ids((1, PAD), 1), node_ids((NEAR, 1), 0)
     for tb in range(4):
         for k in range(2):
-            here = (tb * 2 + k) * 256
+            here = (tb // 2 * 2 + k) * 512 + tb % 2 * 256
             onehot[here : here + 256, :] = jnp.where(
                 ids_t[tb * 256 : tb * 256 + 256, k : k + 1] == across, 1.0, 0.0
             ).astype(BF16)
@@ -151,21 +173,8 @@
                 down == ids[k : k + 1, tb * 256 : tb * 256 + 256], 1.0, 0.0
             ).astype(BF16)
 
-    for load in loads[:4]:
-        load.wait()
-    pl.semaphore_wait(barrier, len(peers))
-
-    def project(c, carry):
-        span = pl.ds(pl.multiple_of(c * CHUNK, CHUNK), CHUNK)
-        near[c, :NODE, :CHUNK] = dot(nodes[...], w_dst[:, span]).astype(BF16)
-        near[c, :NODE, CHUNK:] = dot_cols(cot[...], w_out[span, :]).astype(BF16)
-        for slot in (1, 2, 3, 4):
-            near_copy(c, slot).start()
-        near[c, NEAR:, :] = jnp.zeros((PAD - NEAR, 2 * CHUNK), BF16)
-        return carry
-
-    lax.fori_loop(0, N_CHUNK, project, 0)
-
+    lax.fori_loop(1, N_CHUNK, project_later, 0)
+    send_near(1)
     nodes_t[...] = nodes[...].T
     for load in loads[4:]:
         load.wait()
@@ -182,13 +191,18 @@
         for slot in (1, 2, 3, 4):
             near_copy(c, slot).wait_recv()
 
+        @pl.when(c < N_CHUNK - 2)
+        def _():
+            send_near(c + 2)
+
         def token_block(tb, carry):
-            here = rows(tb * 256, 256)
+            here = rows(tb * 512, 512)
             plain = dot(tokens[here, :], w_src[:, span]) + bias_ref[:, span]
-            total = jnp.zeros((256, CHUNK), F32)
+            total = jnp.zeros((512, CHUNK), F32)
+            both = dot(onehot[rows(tb * 1024, 1024), :], near[c])
             for k in range(2):
-                there = rows((tb * 2 + k) * 256, 256)
-                found = dot(onehot[there, :], near[c])
+                there = rows((tb * 2 + k) * 512, 512)
+                found = both[k * 512 : k * 512 + 512]
                 preact = plain + found[:, :CHUNK]
                 sigma = 0.5 * jnp.tanh(0.5 * preact) + 0.5
                 act = preact * sigma
@@ -197,15 +211,17 @@
                 edges[there, CHUNK:] = grad.astype(BF16)
                 total = total + grad
             back[here, span] = total.astype(BF16)
-            bias_sum[:, span] += jnp.sum(total.reshape(32, 8, CHUNK), axis=0)
+            bias_sum[:, span] += jnp.sum(total.reshape(64, 8, CHUNK), axis=0)
             return carry
 
-        lax.fori_loop(0, 4, token_block, 0, unroll=2)
+        lax.fori_loop(0, 2, token_block, 0, unroll=2)
 
         part[c] = dot(onehot_t[...], edges[...]).astype(BF16)
         for slot in (1, 2, 3, 4):
             part_copy(c, slot).start()
 
+    def source_chunk(c):
+        span = pl.ds(pl.multiple_of(c * CHUNK, CHUNK), CHUNK)
         value = dot(tokens_t[...], back[:, span])
         grads[0, :, :, :, :, span] = value.astype(BF16).reshape(4, 4, 4, 16, CHUNK)
         pair_copy(0, c).start()
@@ -230,12 +246,11 @@
     def pair_add(m, c):
         pair_copy(m, c).wait_recv()
         if m == 2:
-            own = grads[2, c, :, :, :, lanes(core * 512, 512)].astype(F32)
-            acc[2, c] = (own + pair[2, c].astype(F32)).astype(BF16)
+            acc[2, c] = grads[2, c, :, :, :, lanes(core * 512, 512)] + pair[2, c]
             return
         here = lanes(c * 128, 128)
-        own = grads[m, :, :, :, :, lanes(c * CHUNK + core * 128, 128)].astype(F32)
-        acc[m, :, :, :, :, here] = (own + pair[m, :, :, :, :, here].astype(F32)).astype(BF16)
+        own = grads[m, :, :, :, :, lanes(c * CHUNK + core * 128, 128)]
+        acc[m, :, :, :, :, here] = own + pair[m, :, :, :, :, here]
 
     def first_copy(m, c, hop):
         dim = ORDERS[m][0]
@@ -324,24 +339,22 @@
         return remote(fin.at[m, 1 - core], fin_r.at[m], fin_s.at[m], fin_v.at[m], twin)
 
     def chunk(c, carry):
+        @pl.when(c == N_CHUNK - 1)
+        def _():
+            first_send(0, 1)
+            first_send(1, 0)
+            first_send(2, 0)
+
         edge_chunk(c)
 
-        @pl.when(c > 0)
+        @pl.when((c > 0) & (c < N_CHUNK - 1))
         def _():
-            node_chunk(c - 1)
-            first_send(0, c - 1)
-
-        @pl.when(c > 1)
+            source_chunk(c - 1)
+
+        @pl.when(c == N_CHUNK - 2)
         def _():
-            first_send(1, c - 2)
-            first_send(2, c - 2)
-            second_send(0, c - 2)
-
-        @pl.when(c > 2)
-        def _():
-            second_send(1, c - 3)
-            second_send(2, c - 3)
-            second_add(0, c - 3)
+            node_chunk(0)
+            first_send(0, 0)
 
         return carry
 
@@ -377,44 +390,53 @@
     for i in range(8):
         b_acc[0, i : i + 1, :] = jnp.sum(bias_sum[:, i * 128 : i * 128 + 128], axis=0, keepdims=True)
     b_copies = bias_send(0)
+    source_chunk(2)
+    node_chunk(1)
+    source_chunk(3)
+    first_send(0, 2)
+    second_send(0, 0)
+    first_send(1, 1)
+    first_send(2, 1)
+    node_chunk(2)
     first_send(0, 3)
+    second_send(0, 1)
+    b_acc[1] = bias_add(0, b_copies)
+    b_copies = bias_send(1)
+    written = [token_grad_block(0)]
     first_send(1, 2)
     first_send(2, 2)
-    second_send(0, 2)
+    second_send(1, 0)
+    second_send(2, 0)
+    node_chunk(3)
     second_send(1, 1)
     second_send(2, 1)
-    written = [token_grad_block(0)]
-    node_chunk(3)
-    b_acc[1] = bias_add(0, b_copies)
-    b_copies = bias_send(1)
-    written.append(token_grad_block(1))
     first_send(1, 3)
     first_send(2, 3)
+    second_send(0, 2)
     second_send(0, 3)
     second_send(1, 2)
     second_send(2, 2)
     b_acc[2] = bias_add(1, b_copies)
     b_copies = bias_send(2)
-    second_add(0, 1)
-    second_add(0, 2)
-    second_add(1, 0)
-    second_add(2, 0)
-    written.append(token_grad_block(2))
+    written.append(token_grad_block(1))
+    for m in range(3):
+        second_add(m, 0)
+        second_add(m, 1)
     second_send(1, 3)
     second_send(2, 3)
-    second_add(0, 3)
+    for c in (2, 3):
+        second_add(0, c)
     third_send(0)
     b_acc[3] = bias_add(2, b_copies)
     b_copies = bias_send(3)
-    second_add(1, 1)
-    second_add(2, 1)
+    written.append(token_grad_block(2))
     second_add(1, 2)
     second_add(2, 2)
-    written.append(token_grad_block(3))
     second_add(1, 3)
     third_send(1)
     second_add(2, 3)
     third_send(2)
+    written.append(token_grad_block(3))
     updated_ref[...] = (nodes[...].astype(F32) + dot(nsum[...], w_out[...])).astype(BF16)
     node_grad_ref[...] = (cot[...].astype(F32) + dot_cols(nback[...], w_dst[...])).astype(BF16)
     o_bias[...] = bias_add(3, b_copies)

time: 80.9 us -> 74.2 us (0.917)
  Pallas kernels: 79.2 us -> 72.5 us
    pallas_call x1, Pallas kernels: 75 us -> 68.3 us  [body(): pl.pallas_call(layer_kernel, out_shape=(node_like, jax.ShapeDtypeStruct(w...]
where the time goes in v5:
time: 74.2 us; the launch traced here: 74 us
  Pallas kernels  72.5 us (98%)
  between operations  1.45 us (2%)
    pallas_call x1, Pallas kernels, body(): pl.pallas_call(layer_kernel, out_shape=(node_like, jax.ShapeDtypeStruct(w...  68.3 us
    pallas_call x1, Pallas kernels, finish(): pl.pallas_call(finish_kernel, out_shape=(*[jax.ShapeDtypeStruct(a.shape,...  4.19 us

profile of v5, /device:TPU:1, one launch (start us, length us, event | category | flops | bytes accessed | tf_op | source)
XLA Modules:
  0.0 74.0 jit_solution(9622427296914107059)
XLA Ops:
  1.3 68.3 %layer.1 = (bf16[160,1024]{1,0:T(8,128)(2,1)}, bf16[1024,1024]{1,0:T(8,128)(2,1)}, bf16[160,1024]{1,0:T(8,128)(2,1)}, f32[8,1024]{1,0:T(8,128)}, f32[8,1024]{1,0...) custom-call(bf16[1024,1024]{1,0:T(8,128)(2,1)} %tokens_hbm.1, bf16[160,1024]{1,0:T(8,128)(2,1)} %nodes_hbm.1, ...), custom_call_target="tpu_custom_call" | custom-call | tf_op jit(solution)/shard_map/layer/pallas_call | solution.py:531
  69.6 4.2 %finish.1 = (bf16[160,1024]{1,0:T(8,128)(2,1)}, bf16[1024,1024]{1,0:T(8,128)(2,1)}, bf16[160,1024]{1,0:T(8,128)(2,1)}, f32[8,1024]{1,0:T(8,128)}, f32[8,1024]{1,...) custom-call(bf16[160,1024]{1,0:T(8,128)(2,1)} %get-tuple-element.21.refs_0_, ...), custom_call_target="tpu_custom_call" | custom-call | tf_op jit(solution)/shard_map/finish/pallas_call | solution.py:506

commit v6 on v5

--- a/solution.py
+++ b/solution.py
@@ -16,6 +16,7 @@
 ORDERS = ((2, 0, 1), (0, 1, 2), (1, 2, 0))
 BIAS_ORDER = (2, 1, 0)
 HOPS = (2, 1, 3)
+LAST = ((2, True), (2, False), (1, True), (3, True), (1, False), (3, False), (0, True))
 
 
 def device_at(coords, core):
@@ -55,9 +56,9 @@
     updated_ref, token_grad_hbm, node_grad_ref, o_src, o_dst, o_out, o_bias,
     tokens, nodes, w_src, w_dst, w_out, cot, tokens_t, nodes_t, ids, onehot, onehot_t, near, edges,
     back, part, rpart, nsum, nback, grads, stage, bias_sum,
-    acc, pair, r1, r2, r3, fin, fin_r, b_acc, b_r,
+    acc, pair, r1, r2, r3, fin, b_acc, b_r,
     in_sem, out_sem, near_s, near_v, part_s, part_v,
-    pair_s, pair_v, s1, v1, s2, v2, s3, v3, fin_s, fin_v, b_s, b_v,
+    pair_s, pair_v, s1, v1, s2, v2, s3, v3, b_s, b_v,
 ):
     region, sub = lax.axis_index("region"), lax.axis_index("sub")
     n_region, n_sub = 16, 8
@@ -76,6 +77,10 @@
     ]
     facing = (0, 2, 1, 4, 3)
     outs = (o_src, o_dst, o_out)
+    ring_twin = [
+        [device_at(moved(coords, dim, (coords[dim] + hop) % 4), 1 - core) for hop in range(4)]
+        for dim in DIMS
+    ]
     sends = []
 
     def remote(source, target, send, recv, device):
@@ -100,6 +105,7 @@
         load.start()
     barrier = pltpu.get_barrier_semaphore()
     peers = [twin] + ring[0] + ring[1] + ring[2] + around[1:]
+    peers += ring_twin[0][1:] + ring_twin[1][1:] + ring_twin[2][1:]
     for peer in peers:
         pl.semaphore_signal(barrier, inc=1, device_id=peer, device_id_type=MESH)
 
@@ -263,58 +269,64 @@
             target = r1.at[m, hop - 1, :, :, :, here]
         return remote(source, target, s1.at[m, c, hop - 1], v1.at[m, c, hop - 1], ring[dim][hop - 1])
 
-    def second_copy(m, c, hop):
+    def second_copy(m, c, n, hop):
         done, dim = ORDERS[m][:2]
         block = (coords[dim] + hop) % 4
         if m == 2:
-            source, target = acc.at[2, c, coords[done], block], r2.at[2, hop - 1, c]
+            here = pl.ds(c, n)
+            source, target = acc.at[2, here, coords[done], block], r2.at[2, hop - 1, here]
         else:
-            here = lanes(c * 128, 128)
+            here = lanes(c * 128, n * 128)
             source = acc.at[(m, *pick({done: coords[done], dim: block}), slice(None), here)]
             target = r2.at[m, hop - 1, :, :, here]
         return remote(source, target, s2.at[m, c, hop - 1], v2.at[m, c, hop - 1], ring[dim][hop - 1])
 
-    def third_copy(m, hop):
-        one, two, dim = ORDERS[m]
+    def third_copy(m, hop, other):
+        dim = ORDERS[m][2]
         block = (coords[dim] + hop) % 4
-        source = acc.at[(m, *pick({one: coords[one], two: coords[two], dim: block}))]
-        return remote(source, r3.at[m, hop - 1], s3.at[m, hop - 1], v3.at[m, hop - 1], ring[dim][hop - 1])
+        slot = 3 + hop if other else hop - 1
+        device = ring_twin[dim][hop] if other else ring[dim][hop - 1]
+        source = fin.at[m, block, 1 - core if other else core]
+        return remote(source, r3.at[m, slot], s3.at[m, slot], v3.at[m, slot], device)
 
     def first_send(m, c):
         pair_add(m, c)
         for hop in HOPS:
             first_copy(m, c, hop).start()
 
-    def second_send(m, c):
+    def second_send(m, c, n):
         dim = ORDERS[m][0]
-        for hop in HOPS:
-            first_copy(m, c, hop).wait_recv()
-        if m == 2:
-            total = acc[2, c, coords[dim]].astype(F32)
+        for each in range(c, c + n):
+            for hop in HOPS:
+                first_copy(m, each, hop).wait_recv()
+        if m == 2:
+            here = pl.ds(c, n)
+            total = acc[2, here, coords[dim]].astype(F32)
             for slot in range(3):
-                total = total + r1[2, slot, c].astype(F32)
-            acc[2, c, coords[dim]] = total.astype(BF16)
+                total = total + r1[2, slot, here].astype(F32)
+            acc[2, here, coords[dim]] = total.astype(BF16)
         else:
-            here = lanes(c * 128, 128)
+            here = lanes(c * 128, n * 128)
             where = (m, *pick({dim: coords[dim]}), slice(None), here)
             total = acc[where].astype(F32)
             for slot in range(3):
                 total = total + r1[m, slot, :, :, :, here].astype(F32)
             acc[where] = total.astype(BF16)
         for hop in HOPS:
-            second_copy(m, c, hop).start()
-
-    def second_add(m, c):
+            second_copy(m, c, n, hop).start()
+
+    def second_add(m, c, n):
         one, two = ORDERS[m][:2]
         for hop in HOPS:
-            second_copy(m, c, hop).wait_recv()
-        if m == 2:
-            where = (2, c, coords[one], coords[two])
+            second_copy(m, c, n, hop).wait_recv()
+        if m == 2:
+            here = pl.ds(c, n)
+            where = (2, here, coords[one], coords[two])
             total = acc[where].astype(F32)
             for slot in range(3):
-                total = total + r2[2, slot, c].astype(F32)
+                total = total + r2[2, slot, here].astype(F32)
         else:
-            here = lanes(c * 128, 128)
+            here = lanes(c * 128, n * 128)
             where = (m, *pick({one: coords[one], two: coords[two]}), slice(None), here)
             total = acc[where].astype(F32)
             for slot in range(3):
@@ -322,21 +334,18 @@
         acc[where] = total.astype(BF16)
 
     def third_send(m):
-        for hop in HOPS:
-            third_copy(m, hop).start()
-
-    def last_send(m):
-        for hop in HOPS:
-            third_copy(m, hop).wait_recv()
-        total = acc[(m, *coords)].astype(F32)
-        for slot in range(3):
-            total = total + r3[m, slot].astype(F32)
-        fin[m, 0] = total[:8]
-        fin[m, 1] = total[8:]
-        last_copy(m).start()
-
-    def last_copy(m):
-        return remote(fin.at[m, 1 - core], fin_r.at[m], fin_s.at[m], fin_v.at[m], twin)
+        one, two = ORDERS[m][:2]
+        value = acc[(m, *pick({one: coords[one], two: coords[two]}))].astype(F32)
+        fin[m, :, 0] = value[:, :8]
+        fin[m, :, 1] = value[:, 8:]
+        for hop, other in LAST:
+            third_copy(m, hop, other).start()
+
+    def third_add(m):
+        for hop, other in LAST:
+            third_copy(m, hop, other).wait_recv()
+        own = fin[m, coords[ORDERS[m][2]], core]
+        return own + r3[m, 0] + r3[m, 1] + r3[m, 2], r3[m, 3] + r3[m, 4] + r3[m, 5] + r3[m, 6]
 
     def chunk(c, carry):
         @pl.when(c == N_CHUNK - 1)
@@ -394,68 +403,41 @@
     node_chunk(1)
     source_chunk(3)
     first_send(0, 2)
-    second_send(0, 0)
     first_send(1, 1)
     first_send(2, 1)
     node_chunk(2)
     first_send(0, 3)
-    second_send(0, 1)
     b_acc[1] = bias_add(0, b_copies)
     b_copies = bias_send(1)
     written = [token_grad_block(0)]
     first_send(1, 2)
     first_send(2, 2)
-    second_send(1, 0)
-    second_send(2, 0)
     node_chunk(3)
-    second_send(1, 1)
-    second_send(2, 1)
     first_send(1, 3)
     first_send(2, 3)
-    second_send(0, 2)
-    second_send(0, 3)
-    second_send(1, 2)
-    second_send(2, 2)
+    second_send(0, 0, 4)
+    second_send(1, 0, 3)
+    second_send(2, 0, 3)
     b_acc[2] = bias_add(1, b_copies)
     b_copies = bias_send(2)
     written.append(token_grad_block(1))
-    for m in range(3):
-        second_add(m, 0)
-        second_add(m, 1)
-    second_send(1, 3)
-    second_send(2, 3)
-    for c in (2, 3):
-        second_add(0, c)
+    second_send(1, 3, 1)
+    second_send(2, 3, 1)
+    second_add(0, 0, 4)
     third_send(0)
     b_acc[3] = bias_add(2, b_copies)
     b_copies = bias_send(3)
+    second_add(1, 0, 3)
+    second_add(2, 0, 3)
     written.append(token_grad_block(2))
-    second_add(1, 2)
-    second_add(2, 2)
-    second_add(1, 3)
+    second_add(1, 3, 1)
     third_send(1)
-    second_add(2, 3)
+    second_add(2, 3, 1)
     third_send(2)
     written.append(token_grad_block(3))
     updated_ref[...] = (nodes[...].astype(F32) + dot(nsum[...], w_out[...])).astype(BF16)
     node_grad_ref[...] = (cot[...].astype(F32) + dot_cols(nback[...], w_dst[...])).astype(BF16)
     o_bias[...] = bias_add(3, b_copies)
-    for m in range(3):
-        last_send(m)
-    for m in range(3):
-        last_copy(m).wait_recv()
-        if m == 2:
-            outs[m][:, lanes(core * 512, 512)] = fin[m, core]
-            outs[m][:, lanes((1 - core) * 512, 512)] = fin_r[m]
-        else:
-            for c in range(N_CHUNK):
-                part_c = pl.ds(c * 128, 128)
-                outs[m][:, lanes(c * CHUNK + core * 128, 128)] = fin[m, core, :, part_c]
-                outs[m][:, lanes(c * CHUNK + (1 - core) * 128, 128)] = fin_r[m, :, part_c]
-    for copy in written:
-        copy.wait()
-    for copy in sends:
-        copy.wait_send()
 
     def settle(c, carry):
         for slot in (1, 2, 3, 4):
@@ -465,14 +447,31 @@
             pair_copy(m, c).wait_send()
             for hop in HOPS:
                 first_copy(m, c, hop).wait_send()
-                second_copy(m, c, hop).wait_send()
         return carry
 
     lax.fori_loop(0, N_CHUNK, settle, 0)
+    for m, batches in enumerate((((0, 4),), ((0, 3), (3, 1)), ((0, 3), (3, 1)))):
+        for c, n in batches:
+            for hop in HOPS:
+                second_copy(m, c, n, hop).wait_send()
     for m in range(3):
-        last_copy(m).wait_send()
-        for hop in HOPS:
-            third_copy(m, hop).wait_send()
+        own, other = third_add(m)
+        if m == 2:
+            outs[m][:, lanes(core * 512, 512)] = own
+            outs[m][:, lanes((1 - core) * 512, 512)] = other
+        else:
+            for c in range(N_CHUNK):
+                here = slice(c * 128, c * 128 + 128)
+                outs[m][:, lanes(c * CHUNK + core * 128, 128)] = own[:, here]
+                outs[m][:, lanes(c * CHUNK + (1 - core) * 128, 128)] = other[:, here]
+    for copy in written:
+        copy.wait()
+    for copy in sends:
+        copy.wait_send()
+
+    for m in range(3):
+        for hop, other in LAST:
+            third_copy(m, hop, other).wait_send()
 
 
 def finish_kernel(*refs):
@@ -550,14 +549,13 @@
             pltpu.VMEM((3, 4, 4, 4, 16, 512), BF16),
             pltpu.VMEM((3, 3, 4, 4, 16, 512), BF16),
             pltpu.VMEM((3, 3, 4, 16, 512), BF16),
-            pltpu.VMEM((3, 3, 16, 512), BF16),
-            pltpu.VMEM((3, 2, 8, 512), F32),
-            pltpu.VMEM((3, 8, 512), F32),
+            pltpu.VMEM((3, 7, 8, 512), F32),
+            pltpu.VMEM((3, 4, 2, 8, 512), F32),
             pltpu.VMEM((4, 8, 128), F32),
             pltpu.VMEM((10, 8, 128), F32),
             dma((6,)), dma((4,)), dma((4, 4)), dma((4, 4)), dma((4, 4)), dma((4, 4)),
             dma((3, 4)), dma((3, 4)), dma((3, 4, 3)), dma((3, 4, 3)), dma((3, 4, 3)), dma((3, 4, 3)),
-            dma((3, 3)), dma((3, 3)), dma((3,)), dma((3,)), dma((10,)), dma((10,)),
+            dma((3, 7)), dma((3, 7)), dma((10,)), dma((10,)),
         ],
         compiler_params=pltpu.CompilerParams(
             collective_id=1, has_side_effects=True, vmem_limit_bytes=60 * 1024 * 1024

time: 74.2 us -> 72.3 us (0.974)
  Pallas kernels: 72.5 us -> 70.6 us
    pallas_call x1, Pallas kernels: 68.3 us -> 66.5 us  [body(): pl.pallas_call(layer_kernel, out_shape=(node_like, jax.ShapeDtypeStruct(w...]
where the time goes in v6:
time: 72.3 us; the launch traced here: 72.1 us
  Pallas kernels  70.6 us (98%)
  between operations  1.45 us (2%)
    pallas_call x1, Pallas kernels, body(): pl.pallas_call(layer_kernel, out_shape=(node_like, jax.ShapeDtypeStruct(w...  66.5 us
    pallas_call x1, Pallas kernels, finish(): pl.pallas_call(finish_kernel, out_shape=(*[jax.ShapeDtypeStruct(a.shape,...  4.19 us

profile of v6, /device:TPU:1, one launch (start us, length us, event | category | flops | bytes accessed | tf_op | source)
XLA Modules:
  0.0 72.1 jit_solution(12072822036820644036)
XLA Ops:
  1.3 66.5 %layer.1 = (bf16[160,1024]{1,0:T(8,128)(2,1)}, bf16[1024,1024]{1,0:T(8,128)(2,1)}, bf16[160,1024]{1,0:T(8,128)(2,1)}, f32[8,1024]{1,0:T(8,128)}, f32[8,1024]{1,0...) custom-call(bf16[1024,1024]{1,0:T(8,128)(2,1)} %tokens_hbm.1, bf16[160,1024]{1,0:T(8,128)(2,1)} %nodes_hbm.1, ...), custom_call_target="tpu_custom_call" | custom-call | tf_op jit(solution)/shard_map/layer/pallas_call | solution.py:530
  67.7 4.2 %finish.1 = (bf16[160,1024]{1,0:T(8,128)(2,1)}, bf16[1024,1024]{1,0:T(8,128)(2,1)}, bf16[160,1024]{1,0:T(8,128)(2,1)}, f32[8,1024]{1,0:T(8,128)}, f32[8,1024]{1,...) custom-call(bf16[160,1024]{1,0:T(8,128)(2,1)} %get-tuple-element.21.refs_0_, ...), custom_call_target="tpu_custom_call" | custom-call | tf_op jit(solution)/shard_map/finish/pallas_call | solution.py:505

commit v7 on v6

--- a/solution.py
+++ b/solution.py
@@ -16,6 +16,7 @@
 ORDERS = ((2, 0, 1), (0, 1, 2), (1, 2, 0))
 BIAS_ORDER = (2, 1, 0)
 HOPS = (2, 1, 3)
+OWN, TWIN = pl.ds(0, NODE), pl.ds(NODE, NODE)
 LAST = ((2, True), (2, False), (1, True), (3, True), (1, False), (3, False), (0, True))
 
 
@@ -57,7 +58,7 @@
     tokens, nodes, w_src, w_dst, w_out, cot, tokens_t, nodes_t, ids, onehot, onehot_t, near, edges,
     back, part, rpart, nsum, nback, grads, stage, bias_sum,
     acc, pair, r1, r2, r3, fin, b_acc, b_r,
-    in_sem, out_sem, near_s, near_v, part_s, part_v,
+    twin_s, twin_v, in_sem, out_sem, near_s, near_v, part_s, part_v,
     pair_s, pair_v, s1, v1, s2, v2, s3, v3, b_s, b_v,
 ):
     region, sub = lax.axis_index("region"), lax.axis_index("sub")
@@ -97,7 +98,7 @@
     loads = [
         pltpu.make_async_copy(source, target, in_sem.at[i])
         for i, (source, target) in enumerate((
-            (nodes_hbm, nodes), (cot_hbm, cot), (w_dst_hbm, w_dst), (w_out_hbm, w_out),
+            (nodes_hbm, nodes.at[OWN]), (cot_hbm, cot.at[OWN]), (w_dst_hbm, w_dst), (w_out_hbm, w_out),
             (w_src_hbm, w_src), (tokens_hbm, tokens),
         ))
     ]
@@ -121,22 +122,24 @@
             part_s.at[c, facing[slot] - 1], part_v.at[c, facing[slot] - 1], around[slot],
         )
 
+    def twin_copy(i):
+        ref = (nodes, cot)[i]
+        return remote(ref.at[OWN], ref.at[TWIN], twin_s.at[i], twin_v.at[i], twin)
+
     def pair_copy(m, c):
-        if m == 2:
+        if m == 0:
             return remote(
-                grads.at[2, c, :, :, :, lanes((1 - core) * 512, 512)], pair.at[2, c],
-                pair_s.at[2, c], pair_v.at[2, c], twin,
+                grads.at[:, :, :, :, lanes(c * CHUNK + (1 - core) * 128, 128)],
+                pair.at[:, :, :, :, lanes(c * 128, 128)], pair_s.at[0, c], pair_v.at[0, c], twin,
             )
-        return remote(
-            grads.at[m, :, :, :, :, lanes(c * CHUNK + (1 - core) * 128, 128)],
-            pair.at[m, :, :, :, :, lanes(c * 128, 128)],
-            pair_s.at[m, c], pair_v.at[m, c], twin,
-        )
+        ref = (nback, nsum)[m - 1]
+        here = lanes(c * CHUNK + (1 - core) * 128, 128) if m == 1 else lanes(c * CHUNK, CHUNK)
+        return remote(ref.at[OWN, here], ref.at[TWIN, here], pair_s.at[m, c], pair_v.at[m, c], twin)
 
     def project(c):
         span = pl.ds(pl.multiple_of(c * CHUNK, CHUNK), CHUNK)
-        near[c, :NODE, :CHUNK] = dot(nodes[...], w_dst[:, span]).astype(BF16)
-        near[c, :NODE, CHUNK:] = dot_cols(cot[...], w_out[span, :]).astype(BF16)
+        near[c, :NODE, :CHUNK] = dot(nodes[:NODE], w_dst[:, span]).astype(BF16)
+        near[c, :NODE, CHUNK:] = dot_cols(cot[:NODE], w_out[span, :]).astype(BF16)
         near[c, NEAR:, :] = jnp.zeros((PAD - NEAR, 2 * CHUNK), BF16)
 
     def send_near(c):
@@ -154,6 +157,8 @@
     project(0)
     pl.semaphore_wait(barrier, len(peers))
     send_near(0)
+    for i in range(2):
+        twin_copy(i).start()
 
     live = lax.broadcasted_iota(jnp.int32, (2, 1024), 1) < count_ref[...]
     ids[...] = jnp.zeros((8, 1024), jnp.int32)
@@ -181,6 +186,8 @@
 
     lax.fori_loop(1, N_CHUNK, project_later, 0)
     send_near(1)
+    for i in range(2):
+        twin_copy(i).wait_recv()
     nodes_t[...] = nodes[...].T
     for load in loads[4:]:
         load.wait()
@@ -229,7 +236,7 @@
     def source_chunk(c):
         span = pl.ds(pl.multiple_of(c * CHUNK, CHUNK), CHUNK)
         value = dot(tokens_t[...], back[:, span])
-        grads[0, :, :, :, :, span] = value.astype(BF16).reshape(4, 4, 4, 16, CHUNK)
+        grads[:, :, :, :, span] = value.astype(BF16).reshape(4, 4, 4, 16, CHUNK)
         pair_copy(0, c).start()
 
     def node_chunk(c):
@@ -239,24 +246,22 @@
             part_copy(c, facing[slot]).wait_recv()
             total = total + rpart[c, slot - 1].astype(F32)
         total = total.astype(BF16)
-        nsum[:, span] = total[:, :CHUNK]
-        nback[:, span] = total[:, CHUNK:]
-
-        value = dot(nodes_t[...], nback[:, span])
-        grads[1, :, :, :, :, span] = value.astype(BF16).reshape(4, 4, 4, 16, CHUNK)
+        nsum[:NODE, span] = total[:, :CHUNK]
+        nback[:NODE, span] = total[:, CHUNK:]
         pair_copy(1, c).start()
-        value = dot_rows(nsum[:, span], cot[...])
-        grads[2, c] = value.astype(BF16).reshape(4, 4, 16, 1024)
         pair_copy(2, c).start()
 
     def pair_add(m, c):
         pair_copy(m, c).wait_recv()
-        if m == 2:
-            acc[2, c] = grads[2, c, :, :, :, lanes(core * 512, 512)] + pair[2, c]
-            return
-        here = lanes(c * 128, 128)
-        own = grads[m, :, :, :, :, lanes(c * CHUNK + core * 128, 128)]
-        acc[m, :, :, :, :, here] = own + pair[m, :, :, :, :, here]
+        here, mine = lanes(c * 128, 128), lanes(c * CHUNK + core * 128, 128)
+        if m == 0:
+            acc[0, :, :, :, :, here] = grads[:, :, :, :, mine] + pair[:, :, :, :, here]
+        elif m == 1:
+            value = dot(nodes_t[...], nback[:, mine])
+            acc[1, :, :, :, :, here] = value.astype(BF16).reshape(4, 4, 4, 16, 128)
+        else:
+            value = dot_rows(nsum[:, lanes(c * CHUNK, CHUNK)], cot[:, lanes(core * 512, 512)])
+            acc[2, c] = value.astype(BF16).reshape(4, 4, 16, 512)
 
     def first_copy(m, c, hop):
         dim = ORDERS[m][0]
@@ -350,6 +355,7 @@
     def chunk(c, carry):
         @pl.when(c == N_CHUNK - 1)
         def _():
+            node_chunk(1)
             first_send(0, 1)
             first_send(1, 0)
             first_send(2, 0)
@@ -399,19 +405,18 @@
     for i in range(8):
         b_acc[0, i : i + 1, :] = jnp.sum(bias_sum[:, i * 128 : i * 128 + 128], axis=0, keepdims=True)
     b_copies = bias_send(0)
-    source_chunk(2)
-    node_chunk(1)
-    source_chunk(3)
-    first_send(0, 2)
     first_send(1, 1)
     first_send(2, 1)
     node_chunk(2)
+    source_chunk(2)
+    source_chunk(3)
+    first_send(1, 2)
+    first_send(2, 2)
+    first_send(0, 2)
     first_send(0, 3)
     b_acc[1] = bias_add(0, b_copies)
     b_copies = bias_send(1)
     written = [token_grad_block(0)]
-    first_send(1, 2)
-    first_send(2, 2)
     node_chunk(3)
     first_send(1, 3)
     first_send(2, 3)
@@ -435,8 +440,8 @@
     second_add(2, 3, 1)
     third_send(2)
     written.append(token_grad_block(3))
-    updated_ref[...] = (nodes[...].astype(F32) + dot(nsum[...], w_out[...])).astype(BF16)
-    node_grad_ref[...] = (cot[...].astype(F32) + dot_cols(nback[...], w_dst[...])).astype(BF16)
+    updated_ref[...] = (nodes[:NODE].astype(F32) + dot(nsum[:NODE], w_out[...])).astype(BF16)
+    node_grad_ref[...] = (cot[:NODE].astype(F32) + dot_cols(nback[:NODE], w_dst[...])).astype(BF16)
     o_bias[...] = bias_add(3, b_copies)
 
     def settle(c, carry):
@@ -450,6 +455,8 @@
         return carry
 
     lax.fori_loop(0, N_CHUNK, settle, 0)
+    for i in range(2):
+        twin_copy(i).wait_send()
     for m, batches in enumerate((((0, 4),), ((0, 3), (3, 1)), ((0, 3), (3, 1)))):
         for c, n in batches:
             for hop in HOPS:
@@ -536,24 +543,24 @@
         in_specs=[hbm, hbm, vmem, vmem, hbm, hbm, vmem, hbm, hbm],
         out_specs=[vmem, hbm, vmem, vmem, vmem, vmem, vmem],
         scratch_shapes=[
-            pltpu.VMEM(whole, BF16), pltpu.VMEM((NODE, 1024), BF16), pltpu.VMEM(whole, BF16),
-            pltpu.VMEM(whole, BF16), pltpu.VMEM(whole, BF16), pltpu.VMEM((NODE, 1024), BF16),
-            pltpu.VMEM(whole, BF16), pltpu.VMEM((1024, NODE), BF16), pltpu.VMEM((8, 1024), jnp.int32),
+            pltpu.VMEM(whole, BF16), pltpu.VMEM((2 * NODE, 1024), BF16), pltpu.VMEM(whole, BF16),
+            pltpu.VMEM(whole, BF16), pltpu.VMEM(whole, BF16), pltpu.VMEM((2 * NODE, 1024), BF16),
+            pltpu.VMEM(whole, BF16), pltpu.VMEM((1024, 2 * NODE), BF16), pltpu.VMEM((8, 1024), jnp.int32),
             pltpu.VMEM((2048, PAD), BF16), pltpu.VMEM((NEAR, 2048), BF16),
             pltpu.VMEM((N_CHUNK, PAD, 2 * CHUNK), BF16), pltpu.VMEM((2048, 2 * CHUNK), BF16),
             pltpu.VMEM(whole, BF16), pltpu.VMEM((N_CHUNK, NEAR, 2 * CHUNK), BF16),
-            pltpu.VMEM((N_CHUNK, 4, NODE, 2 * CHUNK), BF16), pltpu.VMEM((NODE, 1024), BF16),
-            pltpu.VMEM((NODE, 1024), BF16), pltpu.VMEM((3, 4, 4, 4, 16, 1024), BF16),
+            pltpu.VMEM((N_CHUNK, 4, NODE, 2 * CHUNK), BF16), pltpu.VMEM((2 * NODE, 1024), BF16),
+            pltpu.VMEM((2 * NODE, 1024), BF16), pltpu.VMEM((4, 4, 4, 16, 1024), BF16),
             pltpu.VMEM(whole, BF16), pltpu.VMEM((8, 1024), F32),
             pltpu.VMEM((3, 4, 4, 4, 16, 512), BF16),
-            pltpu.VMEM((3, 4, 4, 4, 16, 512), BF16),
+            pltpu.VMEM((4, 4, 4, 16, 512), BF16),
             pltpu.VMEM((3, 3, 4, 4, 16, 512), BF16),
             pltpu.VMEM((3, 3, 4, 16, 512), BF16),
             pltpu.VMEM((3, 7, 8, 512), F32),
             pltpu.VMEM((3, 4, 2, 8, 512), F32),
             pltpu.VMEM((4, 8, 128), F32),
             pltpu.VMEM((10, 8, 128), F32),
-            dma((6,)), dma((4,)), dma((4, 4)), dma((4, 4)), dma((4, 4)), dma((4, 4)),
+            dma((2,)), dma((2,)), dma((6,)), dma((4,)), dma((4, 4)), dma((4, 4)), dma((4, 4)), dma((4, 4)),
             dma((3, 4)), dma((3, 4)), dma((3, 4, 3)), dma((3, 4, 3)), dma((3, 4, 3)), dma((3, 4, 3)),
             dma((3, 7)), dma((3, 7)), dma((10,)), dma((10,)),
         ],

time: 72.3 us -> 73.4 us (1.015)
  Pallas kernels: 70.6 us -> 71.7 us
    pallas_call x1, Pallas kernels: 66.5 us -> 67.5 us  [body(): pl.pallas_call(layer_kernel, out_shape=(node_like, jax.ShapeDtypeStruct(w...]
where the time goes in v7:
time: 73.4 us; the launch traced here: 73.2 us
  Pallas kernels  71.7 us (98%)
  between operations  1.45 us (2%)
    pallas_call x1, Pallas kernels, body(): pl.pallas_call(layer_kernel, out_shape=(node_like, jax.ShapeDtypeStruct(w...  67.5 us
    pallas_call x1, Pallas kernels, finish(): pl.pallas_call(finish_kernel, out_shape=(*[jax.ShapeDtypeStruct(a.shape,...  4.19 us

profile of v7, /device:TPU:1, one launch (start us, length us, event | category | flops | bytes accessed | tf_op | source)
XLA Modules:
  0.0 73.2 jit_solution(4667164559043166649)
XLA Ops:
  1.3 67.5 %layer.1 = (bf16[160,1024]{1,0:T(8,128)(2,1)}, bf16[1024,1024]{1,0:T(8,128)(2,1)}, bf16[160,1024]{1,0:T(8,128)(2,1)}, f32[8,1024]{1,0:T(8,128)}, f32[8,1024]{1,0...) custom-call(bf16[1024,1024]{1,0:T(8,128)(2,1)} %tokens_hbm.1, bf16[160,1024]{1,0:T(8,128)(2,1)} %nodes_hbm.1, ...), custom_call_target="tpu_custom_call" | custom-call | tf_op jit(solution)/shard_map/layer/pallas_call | solution.py:537
  68.8 4.2 %finish.1 = (bf16[160,1024]{1,0:T(8,128)(2,1)}, bf16[1024,1024]{1,0:T(8,128)(2,1)}, bf16[160,1024]{1,0:T(8,128)(2,1)}, f32[8,1024]{1,0:T(8,128)}, f32[8,1024]{1,...) custom-call(bf16[160,1024]{1,0:T(8,128)(2,1)} %get-tuple-element.21.refs_0_, ...), custom_call_target="tpu_custom_call" | custom-call | tf_op jit(solution)/shard_map/finish/pallas_call | solution.py:512
